TPU v7x, 256 devices: a whole 4x4x8 slice. The times are simulated.
256 devices in a mesh: grp: 8 (over z), dom: 32 (over x, y, core).
Axes of the slice: x: 4, y: 4, z: 8, core: 2. Of those that a mesh axis runs over, the one named last changes fastest.
Arguments:
- hidden_in: bfloat16 [524288, 128], P(('grp', 'dom')), may hold values from -6 to 6
- cotangent: bfloat16 [524288, 128], P(('grp', 'dom')), may hold values from -6 to 6
- coarse_state: bfloat16 [32768, 128], P(('grp', 'dom')), may hold values from -6 to 6
- edge_self: bfloat16 [128, 128], replicated, may hold values from -0.375 to 0.375
- edge_peer: bfloat16 [128, 128], replicated, may hold values from -0.375 to 0.375
- edge_out: bfloat16 [128, 128], replicated, may hold values from -0.1875 to 0.1875
- coarse_self: bfloat16 [128, 128], replicated, may hold values from -0.375 to 0.375
- coarse_peer: bfloat16 [128, 128], replicated, may hold values from -0.375 to 0.375
- coarse_out: bfloat16 [128, 128], replicated, may hold values from -0.1875 to 0.1875
- fine_nbrs: int32 [524288, 8], P(('grp', 'dom')), may hold values from 0 to 2304, as said below
- rim_rows: int32 [65536], P(('grp', 'dom')), may hold values from 0 to 2047, as said below
- send_lists: int32 [8192, 128], P(('grp', 'dom')), may hold values from 0 to 2048, as said below
- member_slots: int32 [8192, 128], P(('grp', 'dom')), may hold values from 0 to 128, as said below
- own_slots: int32 [524288], P(('grp', 'dom')), may hold values from 0 to 128, as said below
- coarse_nbrs: int32 [32768, 8], P(('grp', 'dom')), may hold values from 0 to 128
Outputs:
- hidden_grad: float32 [524288, 128], P(('grp', 'dom'))
- grad_edge_self: float32 [128, 128], replicated
- grad_edge_peer: float32 [128, 128], replicated
- grad_edge_out: float32 [128, 128], replicated
- grad_coarse_self: float32 [128, 128], replicated
- grad_coarse_peer: float32 [128, 128], replicated
- grad_coarse_out: float32 [128, 128], replicated
Inputs may be any that keep to these rules, and one draw needn't show every extreme that they name: `fine_nbrs`: each entry of a fine node's list is a local row of the node's own aligned block of min(512, 2048) rows, a rim row (2048 to 2303), or 2304 for an empty slot. `rim_rows`: distinct local fine rows of the subdomain; the first 128 go to the lower adjacent subdomain, the last 128 to the upper one. `send_lists`: entry 2048 marks an empty slot and fills the tail of each list. A subdomain sends rows only to owners at most two positions away in its group and to the owner 32 // 2 positions away counted round, never to itself; every fine node is sent at most once. Each subdomain sends at most 128 rows to one owner and exactly 128 to one of its adjacent owners. member_slots[o, s, q] is the coarse node of owner o that row send_lists[s, o, q] joins, and 128 exactly where that row is 2048. `own_slots`: 128 exactly for the fine nodes that the subdomain sends away; every coarse node has at least one kept fine node of its own subdomain.
All inputs are finite; a program needn't handle non-finite values.
Results may differ from a plain program's by a relative error of at most 0.007.
Values may be sent and summed in bfloat16 or wider, within the bound.
A program may use at most 64 MiB of HBM per device.

v0:
```python
import jax
import jax.numpy as jnp
from jax import lax
from jax.sharding import PartitionSpec as P


def padded_2(shard, sides, width):
    for axis, dim in sides:
        devices, length = (lax.axis_size(axis), shard.shape[dim])
        up = [(i, (i + 1) % devices) for i in range(devices - 1)]
        down = [(j, i) for i, j in up]
        last = lax.slice_in_dim(shard, length - width, length, axis=dim)
        leading = lax.slice_in_dim(shard, 0, width, axis=dim)
        before = lax.ppermute(last, axis, up)
        after = lax.ppermute(leading, axis, down)
        shard = jnp.concatenate([before, shard, after], axis=dim)
    return shard


def inner_product(left_rows, right_rows):
    return lax.dot_general(
        left_rows, right_rows, (((0,), (0,)), ((), ())), preferred_element_type=jnp.float32
    )


def times_transpose(values, weight):
    return lax.dot_general(
        values, weight, (((1,), (1,)), ((), ())), preferred_element_type=jnp.float32
    )


def exact_transpose(values, weight):
    return lax.dot_general(
        values,
        weight.astype(jnp.float32),
        (((1,), (1,)), ((), ())),
        precision=lax.Precision.HIGHEST,
        preferred_element_type=jnp.float32,
    )


def message_backward(lookup, upstream, neighbors, weight_self, weight_peer, weight_out):
    node_count, slot_count = neighbors.shape
    latent_width = lookup.shape[1]
    pad_row = lookup.shape[0] - 1
    extra_rows = pad_row - node_count
    block_rows = min(512, node_count)
    block_count = node_count // block_rows
    window_width = block_rows + extra_rows
    extras = lookup[node_count:pad_row]
    window_ids = jnp.arange(window_width, dtype=jnp.int32)[None, :]

    def one_block(carried, block_number):
        own_sum, extra_sum, self_grad, grad_self, grad_peer, grad_out = carried
        first_row = block_number * block_rows
        selves = lax.dynamic_slice_in_dim(lookup, first_row, block_rows, 0)
        window = jnp.concatenate([selves, extras], axis=0)
        picked = lax.dynamic_slice_in_dim(neighbors, first_row, block_rows, 0)
        flat_picked = picked.reshape(-1)
        placed = jnp.where(
            flat_picked < node_count,
            flat_picked - first_row,
            jnp.where(flat_picked < pad_row, block_rows + flat_picked - node_count, -1),
        )
        selector = (placed[:, None] == window_ids).astype(jnp.bfloat16)
        peer_rows = jnp.dot(selector, window, preferred_element_type=jnp.float32).astype(
            jnp.bfloat16
        )
        usable = (picked < pad_row).astype(jnp.float32)[:, :, None]
        pre_self = jnp.dot(selves, weight_self, preferred_element_type=jnp.float32)
        pre_peer = jnp.dot(peer_rows, weight_peer, preferred_element_type=jnp.float32).reshape(
            block_rows, slot_count, latent_width
        )
        summed = pre_self[:, None, :] + pre_peer
        squash = jax.nn.sigmoid(summed)
        pooled = jnp.sum(usable * summed * squash, axis=1).astype(jnp.bfloat16)
        arriving = lax.dynamic_slice_in_dim(upstream, first_row, block_rows, 0)
        arriving_b = arriving.astype(jnp.bfloat16)
        grad_out = grad_out + inner_product(pooled, arriving_b)
        grad_pooled = times_transpose(arriving_b, weight_out)
        grad_pre = usable * grad_pooled[:, None, :] * squash * (1.0 + summed * (1.0 - squash))
        grad_pre_b = grad_pre.astype(jnp.bfloat16).reshape(block_rows * slot_count, latent_width)
        grad_sum_b = jnp.sum(grad_pre, axis=1).astype(jnp.bfloat16)
        grad_self = grad_self + inner_product(selves, grad_sum_b)
        grad_peer = grad_peer + inner_product(peer_rows, grad_pre_b)
        to_self = arriving + times_transpose(grad_sum_b, weight_self)
        gathered_sum = inner_product(selector, grad_pre_b)
        own_sum = lax.dynamic_update_slice_in_dim(own_sum, gathered_sum[:block_rows], first_row, 0)
        extra_sum = extra_sum + gathered_sum[block_rows:]
        self_grad = lax.dynamic_update_slice_in_dim(self_grad, to_self, first_row, 0)
        return ((own_sum, extra_sum, self_grad, grad_self, grad_peer, grad_out), None)

    square = jnp.zeros((latent_width, latent_width), jnp.float32)
    initial = (
        jnp.zeros((node_count, latent_width), jnp.float32),
        jnp.zeros((extra_rows, latent_width), jnp.float32),
        jnp.zeros((node_count, latent_width), jnp.float32),
        square,
        square,
        square,
    )
    finished, unused = lax.scan(one_block, initial, jnp.arange(block_count, dtype=jnp.int32))
    own_sum, extra_sum, self_grad, grad_self, grad_peer, grad_out = finished
    return (
        self_grad + exact_transpose(own_sum, weight_peer),
        exact_transpose(extra_sum, weight_peer),
        (grad_self, grad_peer, grad_out),
    )


def far_sum(member_list, arrived, slot_count):
    slot_ids = jnp.arange(slot_count, dtype=jnp.int32)[:, None]
    matches = (member_list.reshape(1, -1) == slot_ids).astype(jnp.bfloat16)
    return jnp.dot(
        matches, arrived.reshape(-1, arrived.shape[-1]), preferred_element_type=jnp.float32
    )


def owner_work(
    local_cot,
    own_list,
    member_list,
    grad_far,
    coarse_rows,
    coarse_links,
    weight_self,
    weight_peer,
    weight_out,
):
    slot_count, latent_width = coarse_rows.shape
    slot_ids = jnp.arange(slot_count, dtype=jnp.int32)[:, None]
    own_match = own_list[None, :] == slot_ids
    far_match = member_list.reshape(1, -1) == slot_ids
    pulled = (
        jnp.dot(own_match.astype(jnp.bfloat16), local_cot, preferred_element_type=jnp.float32)
        + grad_far
    )
    members = (
        jnp.sum(own_match.astype(jnp.int32), axis=1) + jnp.sum(far_match.astype(jnp.int32), axis=1)
    ).astype(jnp.float32)
    zero_row = jnp.zeros((1, latent_width), jnp.bfloat16)
    lookup = jnp.concatenate([coarse_rows, zero_row], axis=0)
    node_grad, unused, grads = message_backward(
        lookup, pulled, coarse_links, weight_self, weight_peer, weight_out
    )
    back_rows = (node_grad / members[:, None]).astype(jnp.bfloat16)
    return (jnp.concatenate([back_rows, zero_row], axis=0), grads)


def fine_grad_in(local_cot, back_rows, own_list, send_list, replies):
    latent_width = local_cot.shape[1]
    upstream = local_cot.astype(jnp.float32) + back_rows[own_list].astype(jnp.float32)
    padded = jnp.concatenate([upstream, jnp.zeros((1, latent_width), jnp.float32)], axis=0)
    padded = padded.at[send_list.reshape(-1)].add(
        replies.reshape(-1, latent_width).astype(jnp.float32)
    )
    return padded[:-1]


def body(
    hidden_in,
    cotangent,
    coarse_state,
    edge_self,
    edge_peer,
    edge_out,
    coarse_self,
    coarse_peer,
    coarse_out,
    fine_nbrs,
    rim_rows,
    send_lists,
    member_slots,
    own_slots,
    coarse_nbrs,
):
    latent_width = hidden_in.shape[1]
    rim_width = rim_rows.shape[0] // 2
    slot_count = coarse_state.shape[0]
    zero_row = jnp.zeros((1, latent_width), jnp.bfloat16)
    cot_padded = jnp.concatenate([cotangent, zero_row], axis=0)
    arrived = lax.all_to_all(cot_padded[send_lists], "dom", split_axis=0, concat_axis=0, tiled=True)
    grad_far = far_sum(member_slots, arrived, slot_count)
    back_rows, coarse_grads = owner_work(
        cotangent,
        own_slots,
        member_slots,
        grad_far,
        coarse_state,
        coarse_nbrs,
        coarse_self,
        coarse_peer,
        coarse_out,
    )
    replies = lax.all_to_all(
        back_rows[member_slots], "dom", split_axis=0, concat_axis=0, tiled=True
    )
    upstream = fine_grad_in(cotangent, back_rows, own_slots, send_lists, replies)
    outgoing = hidden_in[rim_rows]
    widened = padded_2(outgoing, (("dom", 0),), rim_width)
    lookup = jnp.concatenate(
        [hidden_in, widened[:rim_width], widened[-rim_width:], zero_row], axis=0
    )
    node_grad, rim_grad, fine_grads = message_backward(
        lookup, upstream, fine_nbrs, edge_self, edge_peer, edge_out
    )
    returned = padded_2(rim_grad.astype(jnp.bfloat16), (("dom", 0),), rim_width).astype(
        rim_grad.dtype
    )
    hidden_grad = (
        node_grad.at[rim_rows[:rim_width]]
        .add(returned[:rim_width])
        .at[rim_rows[rim_width:]]
        .add(returned[-rim_width:])
    )
    totals = lax.psum(
        (
            fine_grads[0],
            fine_grads[1],
            fine_grads[2],
            coarse_grads[0],
            coarse_grads[1],
            coarse_grads[2],
        ),
        ("grp", "dom"),
    )
    return (hidden_grad, totals[0], totals[1], totals[2], totals[3], totals[4], totals[5])


def solution(mesh):
    in_specs = (
        P(("grp", "dom"), None),
        P(("grp", "dom"), None),
        P(("grp", "dom"), None),
        P(),
        P(),
        P(),
        P(),
        P(),
        P(),
        P(("grp", "dom"), None),
        P(("grp", "dom")),
        P(("grp", "dom"), None),
        P(("grp", "dom"), None),
        P(("grp", "dom")),
        P(("grp", "dom"), None),
    )
    out_specs = (P(("grp", "dom"), None), P(), P(), P(), P(), P(), P())
    return jax.shard_map(body, mesh=mesh, in_specs=in_specs, out_specs=out_specs, check_vma=False)
```

profile of v0, /device:TPU:1, one launch (start us, length us, event | category | flops | bytes accessed | tf_op | source)
XLA Modules:
  0.0 477.1 jit_solution(13188811889824656765)
XLA Ops:
  9.7 4.6 collective-permute-start
  18.1 15.0 %gather_fusion = bf16[4096,128]{1,0:T(8,128)(2,1)} fusion(bf16[2049,128]{1,0:T(8,128)(2,1)S(1)} %concatenate.28, s32[4096]{0:T(1024)S(1)} %fusion.48), kind=kCustom, calls=%fused_computation | custom fusion | bytes 2113536 | tf_op jit(solution)/shard_map/gather | solution.py:182
  33.2 7.8 %all-to-all-start = ((bf16[32,128,128]{2,1,0:T(8,128)(2,1)}), bf16[32,128,128]{2,1,0:T(8,128)(2,1)S(1)}, u32[]{:S(2)}, u32[]{:S(2)}) async-start(bf16[32,128,128]{2,1,0:T(8,128)(2,1)} %bitcast.2), calls=%async_computation | async-start | bytes 2097152 | tf_op jit(solution)/shard_map/all_to_all | solution.py:182
  46.6 11.2 %all-to-all-done = bf16[32,128,128]{2,1,0:T(8,128)(2,1)S(1)} async-done(((bf16[32,128,128]{2,1,0:T(8,128)(2,1)}), bf16[32,128,128]{2,1,0:T(8,128)(2,1)S(1)}, u32[]{:S(2)}, u32[]{:S(2)}) %all-to-all-start) | async-done | bytes 1048608 | tf_op jit(solution)/shard_map/all_to_all | solution.py:182
  61.3 6.2 %gather_fusion.1 = bf16[2048,128]{1,0:T(8,128)(2,1)S(1)} fusion(bf16[129,128]{1,0:T(8,128)(2,1)S(1)} %concatenate.29, s32[2048]{0:T(1024)S(1)} %fusion.56), kind=kCustom, calls=%fused_computation.1 | custom fusion | bytes 1056768 | tf_op jit(solution)/shard_map/gather | solution.py:152
  67.5 15.0 %gather_fusion.2 = bf16[4096,128]{1,0:T(8,128)(2,1)} fusion(bf16[129,128]{1,0:T(8,128)(2,1)S(1)} %concatenate.29, s32[4096]{0:T(1024)S(1)} %copy-done.21), kind=kCustom, calls=%fused_computation.2 | custom fusion | bytes 2113536 | tf_op jit(solution)/shard_map/gather | solution.py:196
  82.5 4.4 all-to-all-start.1
  90.3 13.6 %all-to-all-done.1 = bf16[32,128,128]{2,1,0:T(8,128)(2,1)} async-done(((bf16[32,128,128]{2,1,0:T(8,128)(2,1)}), bf16[32,128,128]{2,1,0:T(8,128)(2,1)}, u32[]{:S(2)}, u32[]{:S(2)}) %all-to-all-start.1) | async-done | bytes 1048608 | tf_op jit(solution)/shard_map/all_to_all | solution.py:195
  104.0 28.9 %scatter_custom_fusion = f32[2049,128]{1,0:T(8,128)S(1)} fusion(f32[2049,128]{1,0:T(8,128)S(1)} %concatenate.30, s32[4096]{0:T(1024)} %bitcast.129, bf16[4096,128]{1,0:T(8,128)(2,1)} %bitcast.17), kind=kCustom, calls=%fused_computation.46 | custom fusion | flops 1048576 | bytes 2097664 | tf_op jit(solution)/shard_map/scatter-add | solution.py:154
  134.2 69.3 %while.8 = (s32[]{:T(128)}, f32[2048,128]{1,0:T(8,128)}, f32[256,128]{1,0:T(8,128)S(1)}, f32[2048,128]{1,0:T(8,128)S(1)}, f32[128,128]{1,0:T(8,128)S(1)}, /*inde...) while((s32[]{:T(128)}, f32[2048,128]{1,0:T(8,128)}, ...), condition=%wide.region_7.8_spmd.clone, body=%wide.region_4.0_spmd.clone.sunk | while | flops 1983381504 | bytes 16318777 | solution.py:102
  138.0 3.0 fusion.136
  143.1 2.9 multiply_reduce_fusion.5
  146.5 4.0 fusion.138
  155.3 3.0 fusion.136
  160.4 2.9 multiply_reduce_fusion.5
  163.8 4.0 fusion.138
  172.6 3.0 fusion.136
  177.7 2.9 multiply_reduce_fusion.5
  181.1 4.0 fusion.138
  190.0 3.0 fusion.136
  195.0 2.9 multiply_reduce_fusion.5
  198.4 4.0 fusion.138
  203.8 2.2 collective-permute-start.2
  214.7 246.5 %all-reduce.6.cloned.1.call-done = (f32[128,128]{1,0:T(8,128)}, f32[128,128]{1,0:T(8,128)}, f32[128,128]{1,0:T(8,128)}, f32[128,128]{0,1:T(8,128)}, f32[128,128]{1,0:T(8,128)}, /*index=5*/f32[128,128]{1,0:T(8,128)}) async-done(((f32[128,128]{1,0:T(8,128)}, f32[128,128]{1,0:T(8,128)}, f32[128,128]{1,0:T(8,128)}, f32[128,128]{0,1:T(8,128)}, f32[128,128]{1,0:T(8,128)}, /*index=5*/f32[128,128]{1,0:T(8,128)}), ...) | async-done | bytes 393232 | tf_op jit(solution)/shard_map/psum | solution.py:216
  (196 shorter events, 63.9 us)
Async XLA Ops:
  7.2 51.6 %copy-start = (bf16[128,128]{1,0:T(8,128)(2,1)S(1)}, bf16[128,128]{1,0:T(8,128)(2,1)}, u32[]{:S(2)}) copy-start(bf16[128,128]{1,0:T(8,128)(2,1)} %param.24) | copy-start | bytes 98308
  9.7 35.0 %collective-permute-start = (bf16[128,128]{1,0:T(8,128)(2,1)S(1)}, bf16[128,128]{1,0:T(8,128)(2,1)S(1)}, u32[]{:S(2)}, u32[]{:S(2)}) collective-permute-start(bf16[128,128]{1,0:T(8,128)(2,1)S(1)} %get-tuple-element.529), channel_id=1, source_target_pairs={{0,1},{1,2},{2,3},{3,4},{4,5},{5,6},{6,7},{7,8},{8,9},{9,10},{10,1... | collective-permute-start | bytes 98312 | tf_op jit(solution)/shard_map/ppermute | solution.py:14
  14.3 30.4 %collective-permute-start.1 = (bf16[128,128]{1,0:T(8,128)(2,1)S(1)}, bf16[128,128]{1,0:T(8,128)(2,1)S(1)}, u32[]{:S(2)}, u32[]{:S(2)}) collective-permute-start(bf16[128,128]{1,0:T(8,128)(2,1)S(1)} %get-tuple-element.530), channel_id=1, source_target_pairs={{1,0},{2,1},{3,2},{4,3},{5,4},{6,5},{7,6},{8,7},{9,8},{10,9},{11,1... | collective-permute-start | bytes 98312 | tf_op jit(solution)/shard_map/ppermute | solution.py:15
  33.1 7.9 %copy-start.29 = (s32[256]{0:T(256)S(1)}, s32[256]{0:T(256)}, u32[]{:S(2)}) copy-start(s32[256]{0:T(256)} %param.27) | copy-start | bytes 3076
  33.1 8.4 %copy-start.27 = (s32[2048]{0:T(1024)S(1)}, s32[2048]{0:T(1024)}, u32[]{:S(2)}) copy-start(s32[2048]{0:T(1024)} %param.30) | copy-start | bytes 24580
  33.1 8.6 %copy-start.28 = (s32[128,8]{0,1:T(8,128)S(1)}, s32[128,8]{0,1:T(8,128)}, u32[]{:S(2)}) copy-start(s32[128,8]{0,1:T(8,128)} %param.31) | copy-start | bytes 12292
  33.1 8.7 %copy-start.24 = (s32[32,128]{1,0:T(8,128)S(1)}, s32[32,128]{1,0:T(8,128)}, u32[]{:S(2)}) copy-start(s32[32,128]{1,0:T(8,128)} %param.29) | copy-start | bytes 49156
  33.1 9.6 %copy-start.23 = (s32[32,128]{1,0:T(8,128)S(1)}, s32[32,128]{1,0:T(8,128)}, u32[]{:S(2)}) copy-start(s32[32,128]{1,0:T(8,128)} %param.28) | copy-start | bytes 49156
  33.1 10.4 %copy-start.15 = (bf16[128,128]{1,0:T(8,128)(2,1)S(1)}, bf16[128,128]{1,0:T(8,128)(2,1)}, u32[]{:S(2)}) copy-start(bf16[128,128]{1,0:T(8,128)(2,1)} %param.19) | copy-start | bytes 98308
  33.1 10.4 %copy-start.17 = (bf16[128,128]{1,0:T(8,128)(2,1)S(1)}, bf16[128,128]{1,0:T(8,128)(2,1)}, u32[]{:S(2)}) copy-start(bf16[128,128]{1,0:T(8,128)(2,1)} %param.23) | copy-start | bytes 98308
  33.1 12.3 %copy-start.5 = (bf16[2048,128]{1,0:T(8,128)(2,1)S(1)}, bf16[2048,128]{1,0:T(8,128)(2,1)}, u32[]{:S(2)}) copy-start(bf16[2048,128]{1,0:T(8,128)(2,1)} %param.17) | copy-start | bytes 1572868
  33.2 24.7 %all-to-all-start = ((bf16[32,128,128]{2,1,0:T(8,128)(2,1)}), bf16[32,128,128]{2,1,0:T(8,128)(2,1)S(1)}, u32[]{:S(2)}, u32[]{:S(2)}) async-start(bf16[32,128,128]{2,1,0:T(8,128)(2,1)} %bitcast.2), calls=%async_computation | async-start | bytes 2097152 | tf_op jit(solution)/shard_map/all_to_all | solution.py:182
  40.9 17.4 %copy-start.6 = (bf16[2048,128]{1,0:T(8,128)(2,1)S(1)}, bf16[2048,128]{1,0:T(8,128)(2,1)}, u32[]{:S(2)}) copy-start(bf16[2048,128]{1,0:T(8,128)(2,1)} %param.18) | copy-start | bytes 1572868
  43.4 15.3 %copy-start.25 = (bf16[128,128]{1,0:T(8,128)(2,1)S(1)}, bf16[128,128]{1,0:T(8,128)(2,1)}, u32[]{:S(2)}) copy-start(bf16[128,128]{1,0:T(8,128)(2,1)} %param.25) | copy-start | bytes 98308
  44.0 16.1 %copy-start.10 = (bf16[1024,128]{1,0:T(8,128)(2,1)}, bf16[1024,128]{1,0:T(8,128)(2,1)S(1)}, u32[]{:S(2)}) copy-start(bf16[1024,128]{1,0:T(8,128)(2,1)S(1)} %convolution_convert_fusion) | copy-start | bytes 786436
  60.5 6.9 %copy-start.8 = (bf16[1024,128]{1,0:T(8,128)(2,1)}, bf16[1024,128]{1,0:T(8,128)(2,1)S(1)}, u32[]{:S(2)}) copy-start(bf16[1024,128]{1,0:T(8,128)(2,1)S(1)} %fusion.30) | copy-start | bytes 786436
  61.3 6.2 %copy-start.21 = (s32[4096]{0:T(1024)S(1)}, s32[4096]{0:T(1024)}, u32[]{:S(2)}) copy-start(s32[4096]{0:T(1024)} %fusion.50) | copy-start | bytes 49156
  82.5 21.4 %all-to-all-start.1 = ((bf16[32,128,128]{2,1,0:T(8,128)(2,1)}), bf16[32,128,128]{2,1,0:T(8,128)(2,1)}, u32[]{:S(2)}, u32[]{:S(2)}) async-start(bf16[32,128,128]{2,1,0:T(8,128)(2,1)} %bitcast.10), calls=%async_computation.1 | async-start | bytes 2097152 | tf_op jit(solution)/shard_map/all_to_all | solution.py:195
  87.0 374.3 %all-reduce.6.cloned.1.call-start = ((), (), s32[]{:S(2)}) async-start(), calls=%async_computation.2 | async-start | bytes 786432 | tf_op jit(solution)/shard_map/psum | solution.py:216
  203.5 4.6 copy-start.2
  203.5 4.6 copy-start.3
  203.8 6.3 %collective-permute-start.2 = (bf16[128,128]{1,0:T(8,128)(2,1)S(1)}, bf16[128,128]{1,0:T(8,128)(2,1)S(1)}, u32[]{:S(2)}, u32[]{:S(2)}) collective-permute-start(bf16[128,128]{1,0:T(8,128)(2,1)S(1)} %get-tuple-element.527), channel_id=1, source_target_pairs={{0,1},{1,2},{2,3},{3,4},{4,5},{5,6},{6,7},{7,8},{8,9},{9,10},{10,1... | collective-permute-start | bytes 98312 | tf_op jit(solution)/shard_map/ppermute | solution.py:14
  205.9 5.2 %collective-permute-start.3 = (bf16[128,128]{1,0:T(8,128)(2,1)S(1)}, bf16[128,128]{1,0:T(8,128)(2,1)S(1)}, u32[]{:S(2)}, u32[]{:S(2)}) collective-permute-start(bf16[128,128]{1,0:T(8,128)(2,1)S(1)} %get-tuple-element.528), channel_id=1, source_target_pairs={{1,0},{2,1},{3,2},{4,3},{5,4},{6,5},{7,6},{8,7},{9,8},{10,9},{11,1... | collective-permute-start | bytes 98312 | tf_op jit(solution)/shard_map/ppermute | solution.py:15
  214.7 255.5 %copy-start.7 = (f32[2048,128]{1,0:T(8,128)}, f32[2048,128]{1,0:T(8,128)S(1)}, u32[]{:S(2)}) copy-start(f32[2048,128]{1,0:T(8,128)S(1)} %scatter_custom_fusion.2) | copy-start | bytes 3145732
  (14 other events, 24.2 us)
Sparse Core Ops, SparseCore 0:
  208.3 252.9 all-reduce.5
where the time goes:
time: 478 us; the launch traced here: 477 us
  waiting for transfers between devices  273 us (57%)
  local copies, waits for them, and re-layouts  64.1 us (13%)
  other arithmetic  51.2 us (11%)
  matrix products  48.4 us (10%)
  starting transfers between devices  23.1 us (5%)
  between operations  14.6 us (3%)
    psum x1, waiting for transfers between devices, body(): lax.psum((fine_grads[0], fine_grads[1], fine_grads[2], coarse_grads[0], c...  247 us
    scatter-add x1, other arithmetic, fine_grad_in(): padded.at[send_list.reshape(-1)]  28.9 us
    dot_general x20, matrix products, inner_product(): lax.dot_general(left_rows, right_rows, (((0,), (0,)), ((), ())), preferre...  23.1 us
    gather x1, local copies, waits for them, and re-layouts, body(): cot_padded[send_lists]  15 us
    gather x1, local copies, waits for them, and re-layouts, body(): back_rows[member_slots]  15 us
    all_to_all x1, waiting for transfers between devices, body(): lax.all_to_all(back_rows[member_slots], 'dom', split_axis=0, concat_axis=...  13.6 us
    dot_general x5, matrix products, one_block(): jnp.dot(selector, window, preferred_element_type=jnp.float32)  12.3 us
    reduce_sum x4, other arithmetic, one_block(): pooled = jnp.sum(usable * summed * squash, axis=1).astype(jnp.bfloat16)  11.7 us
  transfers between devices with their start and end apart: 7, of which 4 were waited for; matrix products, arithmetic and copies ran while one was open for 6% of the time, Pallas kernels for 0%

commit v1 on v0

v1 whole, which is shorter than its diff:
```python
import functools

import jax
import jax.numpy as jnp
from jax import lax
from jax.experimental import pallas as pl
from jax.experimental.pallas import tpu as pltpu
from jax.sharding import PartitionSpec as P

MESH = pl.DeviceIdType.MESH
F32 = jnp.float32
BF16 = jnp.bfloat16
OFF = -1.0e4


def dot(a, b):
    return jnp.dot(a, b, preferred_element_type=F32)


def dot_nt(a, b):
    return lax.dot_general(a, b, (((1,), (1,)), ((), ())), preferred_element_type=F32)


def dot_tn(a, b):
    return lax.dot_general(a, b, (((0,), (0,)), ((), ())), preferred_element_type=F32)


def one_hot(index, shape, axis):
    ids = lax.broadcasted_iota(jnp.int32, shape, axis).astype(jnp.int16)
    hit = jnp.broadcast_to(index.astype(jnp.int16), shape) == ids
    return jnp.where(hit, jnp.ones(shape, BF16), jnp.zeros(shape, BF16))


def in_columns(index, width):
    return one_hot(index, (index.shape[0], width), 1)


def in_rows(index, height):
    return one_hot(index, (height, index.shape[1]), 0)


def split(values):
    high = values.astype(BF16)
    return high, (values - high.astype(F32)).astype(BF16)


def gate(pre):
    squash = 0.5 + 0.5 * jnp.tanh(0.5 * pre)
    act = pre * squash
    return act, squash + act * (1.0 - squash)


def block_kernel(
    n_dom,
    hidden_ref,
    cot_ref,
    coarse_ref,
    ws_ref,
    wp_ref,
    wo_ref,
    cws_ref,
    cwp_ref,
    cwo_ref,
    nbrs_ref,
    rim_ref,
    send_ref,
    member_ref,
    own_ref,
    cnbrs_ref,
    out_ref,
    grads_ref,
    cot_out,
    cot_in,
    rep_out,
    rep_in,
    rim_out,
    rim_in,
    ret_out,
    ret_in,
    peer_hl,
    pre_self_ref,
    window,
    slope_ref,
    pooled_ref,
    own_cols,
    place_ref,
    rim_sum,
    send_sem,
    recv_sem,
):
    grp = lax.axis_index("grp")
    me = lax.axis_index("dom")
    fine, width = hidden_ref.shape
    coarse = coarse_ref.shape[0]
    slots = nbrs_ref.shape[0]
    rim = rim_ref.shape[1]
    sends = send_ref.shape[1]
    block = min(512, fine)
    blocks = fine // block
    span = block + 2 * rim
    offsets = (1, -1, 2, -2, n_dom // 2)
    to = [lax.rem(me + (n_dom + o), n_dom) for o in offsets]
    source = [lax.rem(me + (n_dom - o), n_dom) for o in offsets]

    barrier = pltpu.get_barrier_semaphore()
    for peer in to:
        pl.semaphore_signal(barrier, inc=1, device_id=(grp, peer), device_id_type=MESH)

    def remote(src, dst, index, peer):
        return pltpu.make_async_remote_copy(
            src_ref=src,
            dst_ref=dst,
            send_sem=send_sem.at[index],
            recv_sem=recv_sem.at[index],
            device_id=(grp, peer),
            device_id_type=MESH,
        )

    cot_copies = [remote(cot_out.at[k], cot_in.at[k], k, to[k]) for k in range(5)]
    rim_copies = [remote(rim_out.at[k], rim_in.at[k], 5 + k, to[k]) for k in range(2)]
    rep_copies = [remote(rep_out.at[k], rep_in.at[k], 7 + k, source[k]) for k in range(5)]
    ret_copies = [remote(ret_out.at[k], ret_in.at[k], 12 + k, to[k]) for k in range(2)]

    send_rows = [send_ref[pl.ds(t, 1), :] for t in to]
    member_rows = [member_ref[pl.ds(s, 1), :] for s in source]
    listed = jnp.concatenate(
        send_rows + [rim_ref[1:2, :], rim_ref[0:1, :], jnp.zeros((1, sends), jnp.int32)], axis=0
    )
    listed_cols = listed.T
    for k in range(5):
        cot_out[k] = dot(in_columns(listed_cols[:, k : k + 1], fine), cot_ref[...]).astype(BF16)
    pl.semaphore_wait(barrier, 5)
    for copy in cot_copies:
        copy.start()
    for k in range(2):
        rim_out[k] = dot(in_columns(listed_cols[:, 5 + k : 6 + k], fine), hidden_ref[...]).astype(
            BF16
        )
    for copy in rim_copies:
        copy.start()

    own_cols[...] = own_ref[...].T
    own_hot = jnp.concatenate(
        [in_rows(own_ref[t : t + 1, :], coarse) for t in range(fine // 128)], axis=1
    )
    far_hot = jnp.concatenate([in_rows(row, coarse) for row in member_rows], axis=1)
    own_pull = dot(own_hot, cot_ref[...])
    members = dot(own_hot, jnp.ones((fine, width), BF16)) + dot(
        far_hot, jnp.ones((5 * sends, width), BF16)
    )

    coarse_rows = coarse_ref[...]
    coarse_self = dot(coarse_rows, cws_ref[...])
    coarse_peer = jnp.concatenate(split(dot(coarse_rows, cwp_ref[...])), axis=1)
    links = cnbrs_ref[...]
    link_cols = links.T
    coarse_slopes = []
    coarse_pool = jnp.zeros((coarse, width), F32)
    for j in range(slots):
        col = link_cols[:, j : j + 1]
        got = dot(in_columns(col, coarse), coarse_peer)
        bias = jnp.where(col == coarse, OFF, 0.0)
        act, slope = gate(coarse_self + got[:, :width] + (got[:, width:] + bias))
        coarse_pool += act
        coarse_slopes.append(slope)
    coarse_pool = coarse_pool.astype(BF16)

    both = dot(hidden_ref[...], jnp.concatenate([ws_ref[...], wp_ref[...]], axis=1))
    pre_self_ref[...] = both[:, :width]
    high, low = split(both[:, width:])
    peer_hl[0:fine, 0:width] = high
    peer_hl[0:fine, width:] = low

    for copy in cot_copies:
        copy.wait()
    far_pull = dot(far_hot, cot_in[...].reshape(5 * sends, width))
    pulled = own_pull + far_pull
    pulled_b = pulled.astype(BF16)
    grad_pool = dot_nt(pulled_b, cwo_ref[...])
    grad_sum = jnp.zeros((coarse, width), F32)
    peer_sum = jnp.zeros((coarse, width), F32)
    for j in range(slots):
        grad_pre = grad_pool * coarse_slopes[j]
        grad_sum += grad_pre
        peer_sum += dot(in_rows(links[j : j + 1, :], coarse), grad_pre.astype(BF16))
    grad_sum = grad_sum.astype(BF16)
    high, low = split(peer_sum)
    node_grad = pulled + dot_nt(grad_sum, cws_ref[...])
    node_grad += dot_nt(high, cwp_ref[...]) + dot_nt(low, cwp_ref[...])
    back = (node_grad / members).astype(BF16)
    member_cols = jnp.concatenate(
        member_rows + [jnp.zeros((3, sends), jnp.int32)], axis=0
    ).T
    for k in range(5):
        rep_out[k] = dot(in_columns(member_cols[:, k : k + 1], coarse), back).astype(BF16)
    for copy in rep_copies:
        copy.start()
    grads_ref[3 * width : 4 * width, :] = dot_tn(coarse_rows, grad_sum)
    grads_ref[4 * width : 5 * width, :] = dot_tn(coarse_rows, high) + dot_tn(coarse_rows, low)
    grads_ref[5 * width : 6 * width, :] = dot_tn(coarse_pool, pulled_b)

    for copy in rim_copies:
        copy.wait()
    lower = jnp.where(me > 0, 1.0, 0.0).astype(BF16)
    upper = jnp.where(me < n_dom - 1, 1.0, 0.0).astype(BF16)
    rims = jnp.concatenate([rim_in[0] * lower, rim_in[1] * upper], axis=0)
    high, low = split(dot(rims, wp_ref[...]))
    window[block:, 0:width] = high
    window[block:, width:] = low

    def forward(b, carry):
        first = pl.multiple_of(b * block, block)
        here = pl.ds(first, block)
        picked = nbrs_ref[:, here]
        placed = jnp.where(picked < fine, picked - first, picked - fine + block)
        place_ref[b] = placed
        cols = placed.T
        window[0:block, :] = peer_hl[here, :]
        own_pre = pre_self_ref[here, :]
        total = jnp.zeros((block, width), F32)
        for j in range(slots):
            col = cols[:, j : j + 1]
            got = dot(in_columns(col, span), window[...])
            bias = jnp.where(col == span, OFF, 0.0)
            act, slope = gate(own_pre + got[:, :width] + (got[:, width:] + bias))
            total += act
            slope_ref[b, j] = slope
        pooled_ref[here, :] = total.astype(BF16)
        return carry

    lax.fori_loop(0, blocks, forward, 0)

    for copy in rep_copies:
        copy.wait()
    sources = jnp.concatenate([back, rep_in[...].reshape(5 * sends, width)], axis=0)
    grads_ref[0 : 3 * width, :] = jnp.zeros((3 * width, width), F32)
    rim_sum[...] = jnp.zeros((2 * rim, width), F32)
    self_weight = ws_ref[...]
    peer_weight = wp_ref[...]
    out_weight = wo_ref[...]

    def backward(b, carry):
        first = pl.multiple_of(b * block, block)
        here = pl.ds(first, block)
        own_hots = jnp.concatenate(
            [
                in_columns(own_ref[pl.ds(b * (block // 128) + t, 1), :].T, coarse)
                for t in range(block // 128)
            ],
            axis=0,
        )
        hots = jnp.concatenate([own_hots] + [in_rows(row - first, block) for row in send_rows], axis=1)
        arriving = cot_ref[here, :].astype(F32) + dot(hots, sources)
        arriving_b = arriving.astype(BF16)
        grad_pool = dot_nt(arriving_b, out_weight)
        grad_sum = jnp.zeros((block, width), F32)
        peer_sum = jnp.zeros((span, width), F32)
        placed = place_ref[b]
        for j in range(slots):
            grad_pre = grad_pool * slope_ref[b, j]
            grad_sum += grad_pre
            peer_sum += dot(in_rows(placed[j : j + 1, :], span), grad_pre.astype(BF16))
        grad_sum = grad_sum.astype(BF16)
        rim_sum[...] += peer_sum[block:]
        high, low = split(peer_sum[:block])
        rows = hidden_ref[here, :]
        got = dot_tn(rows, jnp.concatenate([grad_sum, high, low], axis=1))
        grads_ref[0:width, :] += got[:, :width]
        grads_ref[width : 2 * width, :] += got[:, width : 2 * width] + got[:, 2 * width :]
        grads_ref[2 * width : 3 * width, :] += dot_tn(pooled_ref[here, :], arriving_b)
        out_ref[here, :] = (
            arriving
            + dot_nt(grad_sum, self_weight)
            + dot_nt(high, peer_weight)
            + dot_nt(low, peer_weight)
        )
        return carry

    lax.fori_loop(0, blocks, backward, 0)

    high, low = split(rim_sum[...])
    rim_grad = (dot_nt(high, peer_weight) + dot_nt(low, peer_weight)).astype(BF16)
    ret_out[0] = rim_grad[rim:]
    ret_out[1] = rim_grad[:rim]
    for copy in ret_copies:
        copy.start()
    grads_ref[width : 2 * width, :] += dot_tn(rims, high) + dot_tn(rims, low)
    for copy in ret_copies:
        copy.wait()
    returned = jnp.concatenate([ret_in[0] * lower, ret_in[1] * upper], axis=0)

    def give_back(b, carry):
        first = pl.multiple_of(b * block, block)
        here = pl.ds(first, block)
        hots = jnp.concatenate([in_rows(rim_ref[k : k + 1, :] - first, block) for k in range(2)], axis=1)
        out_ref[here, :] += dot(hots, returned)
        return carry

    lax.fori_loop(0, blocks, give_back, 0)


def sum_kernel(n_grp, n_dom, part_ref, out_ref, first_in, mine, second_in, send_sem, recv_sem):
    grp = lax.axis_index("grp")
    dom = lax.axis_index("dom")
    plane = n_dom // 2
    column = n_grp * 2
    core = lax.rem(dom, 2)
    place = dom // 2
    level = grp * 2 + core
    rows = part_ref.shape[0] // plane

    def in_plane(index):
        return (grp, index * 2 + core)

    def in_column(index):
        return (index // 2, place * 2 + lax.rem(index, 2))

    barrier = pltpu.get_barrier_semaphore()
    for t in range(1, plane):
        pl.semaphore_signal(
            barrier, inc=1, device_id=in_plane(lax.rem(place + t, plane)), device_id_type=MESH
        )
    for t in range(1, column):
        pl.semaphore_signal(
            barrier, inc=1, device_id=in_column(lax.rem(level + t, column)), device_id_type=MESH
        )
    pl.semaphore_wait(barrier, plane + column - 2)

    def cut(index):
        return pl.ds(pl.multiple_of(index * rows, 8), rows)

    def copy(src, dst, index, peer):
        return pltpu.make_async_remote_copy(
            src_ref=src,
            dst_ref=dst,
            send_sem=send_sem.at[index],
            recv_sem=recv_sem.at[index],
            device_id=peer,
            device_id_type=MESH,
        )

    def ahead(t):
        return lax.rem(place + t, plane)

    first = [
        copy(part_ref.at[cut(ahead(t)), :], first_in.at[place], t, in_plane(ahead(t)))
        for t in range(1, plane)
    ]
    for c in first:
        c.start()
    first_in[place] = part_ref[cut(place), :]
    for c in first:
        c.wait()
    total = first_in[0]
    for t in range(1, plane):
        total += first_in[t]
    mine[...] = total
    second = [
        copy(mine, second_in.at[level], plane + t, in_column(lax.rem(level + t, column)))
        for t in range(1, column)
    ]
    for c in second:
        c.start()
    second_in[level] = total
    for c in second:
        c.wait()
    total = second_in[0]
    for t in range(1, column):
        total += second_in[t]
    out_ref[cut(place), :] = total
    third = [
        copy(
            out_ref.at[cut(place), :],
            out_ref.at[cut(place), :],
            plane + column + t,
            in_plane(ahead(t)),
        )
        for t in range(1, plane)
    ]
    for c in third:
        c.start()
    for c in third:
        c.wait()


def finish_kernel(node_ref, sums_ref, out_ref, *rest):
    parts, sem = rest[:-1], rest[-1]
    width = sums_ref.shape[1]
    copies = [pltpu.make_async_copy(node_ref, out_ref, sem.at[6])]
    for k, part in enumerate(parts):
        copies.append(
            pltpu.make_async_copy(sums_ref.at[pl.ds(k * width, width), :], part, sem.at[k])
        )
    for copy in copies:
        copy.start()
    for copy in copies:
        copy.wait()


def body(
    n_grp,
    n_dom,
    hidden_in,
    cotangent,
    coarse_state,
    edge_self,
    edge_peer,
    edge_out,
    coarse_self,
    coarse_peer,
    coarse_out,
    fine_nbrs,
    rim_rows,
    send_lists,
    member_slots,
    own_slots,
    coarse_nbrs,
):
    fine, width = hidden_in.shape
    coarse = coarse_state.shape[0]
    slots = fine_nbrs.shape[1]
    rim = rim_rows.shape[0] // 2
    sends = send_lists.shape[1]
    block = min(512, fine)
    blocks = fine // block
    vmem = pl.BlockSpec(memory_space=pltpu.VMEM)
    node_grad, grads = pl.pallas_call(
        functools.partial(block_kernel, n_dom),
        out_shape=(
            jax.ShapeDtypeStruct((fine, width), F32),
            jax.ShapeDtypeStruct((6 * width, width), F32),
        ),
        in_specs=[vmem] * 15,
        out_specs=(vmem, vmem),
        scratch_shapes=[
            pltpu.VMEM((5, sends, width), BF16),
            pltpu.VMEM((5, sends, width), BF16),
            pltpu.VMEM((5, sends, width), BF16),
            pltpu.VMEM((5, sends, width), BF16),
            pltpu.VMEM((2, rim, width), BF16),
            pltpu.VMEM((2, rim, width), BF16),
            pltpu.VMEM((2, rim, width), BF16),
            pltpu.VMEM((2, rim, width), BF16),
            pltpu.VMEM((fine, 2 * width), BF16),
            pltpu.VMEM((fine, width), F32),
            pltpu.VMEM((block + 2 * rim, 2 * width), BF16),
            pltpu.VMEM((blocks, slots, block, width), F32),
            pltpu.VMEM((fine, width), BF16),
            pltpu.VMEM((128, fine // 128), jnp.int32),
            pltpu.VMEM((blocks, slots, block), jnp.int32),
            pltpu.VMEM((2 * rim, width), F32),
            pltpu.SemaphoreType.DMA((14,)),
            pltpu.SemaphoreType.DMA((14,)),
        ],
        compiler_params=pltpu.CompilerParams(
            collective_id=0, has_side_effects=True, vmem_limit_bytes=48 * 1024 * 1024
        ),
        name="block",
    )(
        hidden_in,
        cotangent,
        coarse_state,
        edge_self,
        edge_peer,
        edge_out,
        coarse_self,
        coarse_peer,
        coarse_out,
        fine_nbrs.T,
        rim_rows.reshape(2, rim),
        send_lists,
        member_slots,
        own_slots.reshape(fine // 128, 128),
        coarse_nbrs.T,
    )
    plane, column = n_dom // 2, n_grp * 2
    rows = 6 * width // plane
    sums = pl.pallas_call(
        functools.partial(sum_kernel, n_grp, n_dom),
        out_shape=jax.ShapeDtypeStruct((6 * width, width), F32),
        in_specs=[vmem],
        out_specs=vmem,
        scratch_shapes=[
            pltpu.VMEM((plane, rows, width), F32),
            pltpu.VMEM((rows, width), F32),
            pltpu.VMEM((column, rows, width), F32),
            pltpu.SemaphoreType.DMA((2 * plane + column,)),
            pltpu.SemaphoreType.DMA((2 * plane + column,)),
        ],
        compiler_params=pltpu.CompilerParams(
            collective_id=1, has_side_effects=True, vmem_limit_bytes=16 * 1024 * 1024
        ),
        name="sums",
    )(grads)
    anywhere = pl.BlockSpec(memory_space=pl.ANY)
    square = jax.ShapeDtypeStruct((width, width), F32)
    return pl.pallas_call(
        finish_kernel,
        out_shape=(jax.ShapeDtypeStruct((fine, width), F32),) + (square,) * 6,
        in_specs=[anywhere] * 2,
        out_specs=(anywhere,) * 7,
        scratch_shapes=[pltpu.SemaphoreType.DMA((7,))],
        name="finish",
    )(node_grad, sums)


def solution(mesh):
    rows = P(("grp", "dom"), None)
    flat = P(("grp", "dom"))
    whole = P()
    in_specs = (rows,) * 3 + (whole,) * 6 + (rows, flat, rows, rows, flat, rows)
    out_specs = (rows,) + (whole,) * 6
    return jax.shard_map(
        functools.partial(body, mesh.shape["grp"], mesh.shape["dom"]),
        mesh=mesh,
        in_specs=in_specs,
        out_specs=out_specs,
        check_vma=False,
    )
```

time: 478 us -> 131 us (0.27)
  waiting for transfers between devices: 273 us -> 0 us
  Pallas kernels: 0 us -> 117 us
  local copies, waits for them, and re-layouts: 64.1 us -> 12.8 us
  other arithmetic: 51.2 us -> 0 us
  matrix products: 48.4 us -> 0 us
  starting transfers between devices: 23.1 us -> 0 us
  between operations: 14.6 us -> 0.7 us
    psum x1 -> x0, waiting for transfers between devices: 247 us -> none  [body(): lax.psum((fine_grads[0], fine_grads[1], fine_grads[2], coarse_grads[0], c...]
    pallas_call x0 -> x3, Pallas kernels: none -> 117 us  [the longest x1 44.8 us: body(): pl.pallas_call(finish_kernel, out_shape=(jax.ShapeDtypeStruct((fine, widt...]
    dot_general x50 -> x0, matrix products: 48.4 us -> none  [the longest x20 23.1 us: inner_product(): lax.dot_general(left_rows, right_rows, (((0,), (0,)), ((), ())), preferre...]
    gather x4 -> x0, local copies, waits for them, and re-layouts: 38.1 us -> none  [the longest x1 15 us: body(): cot_padded[send_lists]]
    scatter-add x3 -> x0, other arithmetic: 32.5 us -> none  [the longest x1 28.9 us: fine_grad_in(): padded.at[send_list.reshape(-1)]]
    all_to_all x2 -> x0, waiting for transfers between devices: 24.9 us -> none  [the longest x1 13.6 us: body(): lax.all_to_all(back_rows[member_slots], 'dom', split_axis=0, concat_axis=...]
    all_to_all x2 -> x0, starting transfers between devices: 12.2 us -> none  [the longest x1 7.78 us: body(): lax.all_to_all(cot_padded[send_lists], 'dom', split_axis=0, concat_axis=0...]
    reduce_sum x6 -> x0, other arithmetic: 12.1 us -> none  [the longest x4 11.7 us: one_block(): pooled = jnp.sum(usable * summed * squash, axis=1).astype(jnp.bfloat16)]
  transfers between devices with their start and end apart: 7 -> 0, of which waited for: 4 -> 0; matrix products, arithmetic and copies ran while one was open for 6% -> 0% of each run, Pallas kernels for 0% -> 0%
where the time goes in v1:
time: 131 us; the launch traced here: 130 us
  Pallas kernels  117 us (89%)
  local copies, waits for them, and re-layouts  12.8 us (10%)
    pallas_call x1, Pallas kernels, body(): pl.pallas_call(finish_kernel, out_shape=(jax.ShapeDtypeStruct((fine, widt...  44.8 us
    pallas_call x1, Pallas kernels, body(): pl.pallas_call(functools.partial(block_kernel, n_dom), out_shape=(jax.Sha...  36.9 us
    pallas_call x1, Pallas kernels, body(): pl.pallas_call(functools.partial(sum_kernel, n_grp, n_dom), out_shape=jax...  35.1 us
    unnamed x34, local copies, waits for them, and re-layouts  12.8 us

profile of v1, /device:TPU:1, one launch (start us, length us, event | category | flops | bytes accessed | tf_op | source)
XLA Modules:
  0.0 130.3 jit_solution(8267149094694463454)
XLA Ops:
  0.6 0.0 copy-start.15
  0.6 0.0 copy-start.16
  0.7 0.7 copy-done.15
  1.3 0.0 copy-done.16
  1.3 1.0 copy-done.2
  2.4 1.0 copy-done.3
  3.4 0.8 copy-done.4
  4.3 0.8 copy-done.5
  5.0 0.8 copy-done.6
  5.8 0.8 copy-done.7
  6.5 0.8 copy-done.8
  7.3 0.8 copy-done.9
  8.1 0.8 copy-done.10
  8.8 0.8 copy-done.11
  9.6 0.7 copy-done.12
  10.3 0.7 copy-done.13
  11.0 0.7 copy-done.14
  11.7 36.9 %block.1 = (f32[2048,128]{1,0:T(8,128)S(1)}, f32[768,128]{1,0:T(8,128)S(1)}) custom-call(bf16[2048,128]{1,0:T(8,128)(2,1)S(1)} %copy-done.2, bf16[2048,128]{1,0:T(8,128)(2,1)S(1)} %copy-done.3, bf16[128,128]{1,0:T(8,128)(2,1)S(1)} %copy-done.5, bf16[128,128]{1,0:T(8,128)(2,1)S(1)} %copy-done.6, bf16[128,128]{1,0:T(8,128)(2,1)S(1)} %copy-done.7, ...), custom_call_target="tpu_custom_call" | custom-call | tf_op jit(solution)/shard_map/block/pallas_call | solution.py:427
  48.6 0.0 copy-start.1
  48.6 1.0 copy-done.1
  49.6 35.1 %sums.1.sums_ref = f32[768,128]{1,0:T(8,128)S(1)} custom-call(f32[768,128]{1,0:T(8,128)S(1)} %get-tuple-element.10.part_ref), custom_call_target="tpu_custom_call" | custom-call | tf_op jit(solution)/shard_map/sums/pallas_call | solution.py:478
  84.7 0.0 copy-start
  84.7 0.8 copy-done
  85.5 44.8 %finish.1 = (f32[2048,128]{1,0:T(8,128)}, f32[128,128]{1,0:T(8,128)}, f32[128,128]{1,0:T(8,128)}, f32[128,128]{1,0:T(8,128)}, f32[128,128]{1,0:T(8,128)}, /*index=5*/f32[128,128]{1,0:T(8,128)}, f32[128,128]{1,0:T(8,128)}) custom-call(f32[2048,128]{1,0:T(8,128)} %copy-done.1, f32[768,128]{1,0:T(8,128)} %copy-done), custom_call_target="tpu_custom_call" | custom-call | tf_op jit(solution)/shard_map/finish/pallas_call | solution.py:497
  (13 shorter events, 0.0 us)
Async XLA Ops:
  0.6 0.7 copy-start.15
  0.6 0.7 copy-start.16
  1.3 1.0 copy-start.2
  2.4 1.0 copy-start.3
  3.4 0.8 copy-start.4
  4.3 0.8 copy-start.5
  5.0 0.8 copy-start.6
  5.8 0.8 copy-start.7
  6.5 0.8 copy-start.8
  7.3 0.8 copy-start.9
  8.1 0.8 copy-start.10
  8.8 0.8 copy-start.11
  9.6 0.7 copy-start.12
  10.3 0.7 copy-start.13
  11.0 0.7 copy-start.14
  48.6 1.0 copy-start.1
  84.7 0.8 copy-start

commit v2 on v1

--- a/solution.py
+++ b/solution.py
@@ -50,44 +50,67 @@
     return act, squash + act * (1.0 - squash)
 
 
-def block_kernel(
-    n_dom,
-    hidden_ref,
-    cot_ref,
-    coarse_ref,
-    ws_ref,
-    wp_ref,
-    wo_ref,
-    cws_ref,
-    cwp_ref,
-    cwo_ref,
-    nbrs_ref,
-    rim_ref,
-    send_ref,
-    member_ref,
-    own_ref,
-    cnbrs_ref,
-    out_ref,
-    grads_ref,
-    cot_out,
-    cot_in,
-    rep_out,
-    rep_in,
-    rim_out,
-    rim_in,
-    ret_out,
-    ret_in,
-    peer_hl,
-    pre_self_ref,
-    window,
-    slope_ref,
-    pooled_ref,
-    own_cols,
-    place_ref,
-    rim_sum,
-    send_sem,
-    recv_sem,
-):
+NAMES = 15
+
+
+def block_kernel(n_grp, n_dom, *refs):
+    inputs = refs[:NAMES]
+    out_ref, grads_ref = refs[NAMES : NAMES + 2]
+    held = refs[NAMES + 2 : 2 * NAMES + 2]
+    (
+        cot_out,
+        cot_in,
+        rep_out,
+        rep_in,
+        rim_out,
+        rim_in,
+        ret_out,
+        ret_in,
+        peer_hl,
+        pre_self_ref,
+        window,
+        slope_ref,
+        pooled_ref,
+        place_ref,
+        rim_sum,
+        part_ref,
+        first_a,
+        first_b,
+        mine_a,
+        mine_b,
+        second_a,
+        second_b,
+        load_sem,
+        send_sem,
+        recv_sem,
+        sum_send,
+        sum_recv,
+    ) = refs[2 * NAMES + 2 :]
+    (
+        hidden_ref,
+        cot_ref,
+        coarse_ref,
+        ws_ref,
+        wp_ref,
+        wo_ref,
+        cws_ref,
+        cwp_ref,
+        cwo_ref,
+        nbrs_ref,
+        rim_ref,
+        send_ref,
+        member_ref,
+        own_ref,
+        cnbrs_ref,
+    ) = held
+    loads = [
+        pltpu.make_async_copy(src, dst, load_sem.at[i])
+        for i, (src, dst) in enumerate(zip(inputs, held))
+    ]
+    order = (11, 1, 10, 0, 12, 13, 2, 6, 7, 8, 14, 3, 4, 5, 9)
+    for i in order:
+        loads[i].start()
+
     grp = lax.axis_index("grp")
     me = lax.axis_index("dom")
     fine, width = hidden_ref.shape
@@ -103,8 +126,19 @@
     source = [lax.rem(me + (n_dom - o), n_dom) for o in offsets]
 
     barrier = pltpu.get_barrier_semaphore()
-    for peer in to:
-        pl.semaphore_signal(barrier, inc=1, device_id=(grp, peer), device_id_type=MESH)
+
+    def greet_dom(t, carry):
+        peer = (grp, lax.rem(me + t, n_dom))
+        pl.semaphore_signal(barrier, inc=1, device_id=peer, device_id_type=MESH)
+        return carry
+
+    def greet_grp(t, carry):
+        peer = (lax.rem(grp + t, n_grp), me)
+        pl.semaphore_signal(barrier, inc=1, device_id=peer, device_id_type=MESH)
+        return carry
+
+    lax.fori_loop(1, n_dom, greet_dom, 0)
+    lax.fori_loop(1, n_grp, greet_grp, 0)
 
     def remote(src, dst, index, peer):
         return pltpu.make_async_remote_copy(
@@ -121,25 +155,96 @@
     rep_copies = [remote(rep_out.at[k], rep_in.at[k], 7 + k, source[k]) for k in range(5)]
     ret_copies = [remote(ret_out.at[k], ret_in.at[k], 12 + k, to[k]) for k in range(2)]
 
+    class Sum:
+        def __init__(self, base, size, first, mine, second, sems):
+            self.base, self.rows = base, size // n_dom
+            self.first, self.mine, self.second, self.sems = first, mine, second, sems
+
+        def copy(self, src, dst, index, peer):
+            return pltpu.make_async_remote_copy(
+                src_ref=src,
+                dst_ref=dst,
+                send_sem=sum_send.at[self.sems + index],
+                recv_sem=sum_recv.at[self.sems + index],
+                device_id=peer,
+                device_id_type=MESH,
+            )
+
+        def cut(self, index):
+            return pl.ds(pl.multiple_of(self.base + index * self.rows, 8), self.rows)
+
+        def scatter(self, t):
+            peer = lax.rem(me + t, n_dom)
+            return self.copy(
+                part_ref.at[self.cut(peer), :], self.first.at[me], t, (grp, peer)
+            )
+
+        def across(self, t):
+            peer = lax.rem(grp + t, n_grp)
+            return self.copy(self.mine, self.second.at[grp], n_dom + t, (peer, me))
+
+        def gather(self, t):
+            peer = lax.rem(me + t, n_dom)
+            mine = grads_ref.at[self.cut(me), :]
+            return self.copy(mine, mine, n_dom + n_grp + t, (grp, peer))
+
+        def each(self, make, count, act):
+            def step(t, carry):
+                act(make(t))
+                return carry
+
+            lax.fori_loop(1, count, step, 0)
+
+        def start_scatter(self):
+            self.each(self.scatter, n_dom, lambda c: c.start())
+            self.first[me] = part_ref[self.cut(me), :]
+
+        def start_across(self):
+            self.each(self.scatter, n_dom, lambda c: c.wait())
+            total = self.first[0]
+            for t in range(1, n_dom):
+                total += self.first[t]
+            self.mine[...] = total
+            self.each(self.across, n_grp, lambda c: c.start())
+            self.second[grp] = total
+
+        def start_gather(self):
+            self.each(self.across, n_grp, lambda c: c.wait())
+            total = self.second[0]
+            for t in range(1, n_grp):
+                total += self.second[t]
+            grads_ref[self.cut(me), :] = total
+            self.each(self.gather, n_dom, lambda c: c.start())
+
+        def finish(self):
+            self.each(self.gather, n_dom, lambda c: c.wait())
+
+    sum_a = Sum(2 * width, 4 * width, first_a, mine_a, second_a, 0)
+    sum_b = Sum(0, 2 * width, first_b, mine_b, second_b, 2 * n_dom + n_grp)
+
+    for i in (11, 10, 1):
+        loads[i].wait()
     send_rows = [send_ref[pl.ds(t, 1), :] for t in to]
-    member_rows = [member_ref[pl.ds(s, 1), :] for s in source]
     listed = jnp.concatenate(
         send_rows + [rim_ref[1:2, :], rim_ref[0:1, :], jnp.zeros((1, sends), jnp.int32)], axis=0
     )
     listed_cols = listed.T
     for k in range(5):
         cot_out[k] = dot(in_columns(listed_cols[:, k : k + 1], fine), cot_ref[...]).astype(BF16)
-    pl.semaphore_wait(barrier, 5)
+    pl.semaphore_wait(barrier, n_dom + n_grp - 2)
     for copy in cot_copies:
         copy.start()
+    loads[0].wait()
     for k in range(2):
         rim_out[k] = dot(in_columns(listed_cols[:, 5 + k : 6 + k], fine), hidden_ref[...]).astype(
             BF16
         )
     for copy in rim_copies:
         copy.start()
-
-    own_cols[...] = own_ref[...].T
+    for i in range(NAMES):
+        if i not in (0, 1, 10, 11):
+            loads[i].wait()
+    member_rows = [member_ref[pl.ds(s, 1), :] for s in source]
     own_hot = jnp.concatenate(
         [in_rows(own_ref[t : t + 1, :], coarse) for t in range(fine // 128)], axis=1
     )
@@ -195,9 +300,9 @@
         rep_out[k] = dot(in_columns(member_cols[:, k : k + 1], coarse), back).astype(BF16)
     for copy in rep_copies:
         copy.start()
-    grads_ref[3 * width : 4 * width, :] = dot_tn(coarse_rows, grad_sum)
-    grads_ref[4 * width : 5 * width, :] = dot_tn(coarse_rows, high) + dot_tn(coarse_rows, low)
-    grads_ref[5 * width : 6 * width, :] = dot_tn(coarse_pool, pulled_b)
+    part_ref[3 * width : 4 * width, :] = dot_tn(coarse_rows, grad_sum)
+    part_ref[4 * width : 5 * width, :] = dot_tn(coarse_rows, high) + dot_tn(coarse_rows, low)
+    part_ref[5 * width : 6 * width, :] = dot_tn(coarse_pool, pulled_b)
 
     for copy in rim_copies:
         copy.wait()
@@ -233,13 +338,13 @@
     for copy in rep_copies:
         copy.wait()
     sources = jnp.concatenate([back, rep_in[...].reshape(5 * sends, width)], axis=0)
-    grads_ref[0 : 3 * width, :] = jnp.zeros((3 * width, width), F32)
+    part_ref[0 : 3 * width, :] = jnp.zeros((3 * width, width), F32)
     rim_sum[...] = jnp.zeros((2 * rim, width), F32)
     self_weight = ws_ref[...]
     peer_weight = wp_ref[...]
     out_weight = wo_ref[...]
 
-    def backward(b, carry):
+    def arrive(b, carry):
         first = pl.multiple_of(b * block, block)
         here = pl.ds(first, block)
         own_hots = jnp.concatenate(
@@ -251,8 +356,18 @@
         )
         hots = jnp.concatenate([own_hots] + [in_rows(row - first, block) for row in send_rows], axis=1)
         arriving = cot_ref[here, :].astype(F32) + dot(hots, sources)
-        arriving_b = arriving.astype(BF16)
-        grad_pool = dot_nt(arriving_b, out_weight)
+        out_ref[here, :] = arriving
+        part_ref[2 * width : 3 * width, :] += dot_tn(pooled_ref[here, :], arriving.astype(BF16))
+        return carry
+
+    lax.fori_loop(0, blocks, arrive, 0)
+    sum_a.start_scatter()
+
+    def backward(b, carry):
+        first = pl.multiple_of(b * block, block)
+        here = pl.ds(first, block)
+        arriving = out_ref[here, :]
+        grad_pool = dot_nt(arriving.astype(BF16), out_weight)
         grad_sum = jnp.zeros((block, width), F32)
         peer_sum = jnp.zeros((span, width), F32)
         placed = place_ref[b]
@@ -265,9 +380,8 @@
         high, low = split(peer_sum[:block])
         rows = hidden_ref[here, :]
         got = dot_tn(rows, jnp.concatenate([grad_sum, high, low], axis=1))
-        grads_ref[0:width, :] += got[:, :width]
-        grads_ref[width : 2 * width, :] += got[:, width : 2 * width] + got[:, 2 * width :]
-        grads_ref[2 * width : 3 * width, :] += dot_tn(pooled_ref[here, :], arriving_b)
+        part_ref[0:width, :] += got[:, :width]
+        part_ref[width : 2 * width, :] += got[:, width : 2 * width] + got[:, 2 * width :]
         out_ref[here, :] = (
             arriving
             + dot_nt(grad_sum, self_weight)
@@ -276,15 +390,21 @@
         )
         return carry
 
-    lax.fori_loop(0, blocks, backward, 0)
+    half = max(blocks // 2, 1)
+    lax.fori_loop(0, half, backward, 0)
+    sum_a.start_across()
+    lax.fori_loop(half, blocks, backward, 0)
+    sum_a.start_gather()
 
     high, low = split(rim_sum[...])
+    part_ref[width : 2 * width, :] += dot_tn(rims, high) + dot_tn(rims, low)
+    sum_b.start_scatter()
     rim_grad = (dot_nt(high, peer_weight) + dot_nt(low, peer_weight)).astype(BF16)
     ret_out[0] = rim_grad[rim:]
     ret_out[1] = rim_grad[:rim]
     for copy in ret_copies:
         copy.start()
-    grads_ref[width : 2 * width, :] += dot_tn(rims, high) + dot_tn(rims, low)
+    sum_b.start_across()
     for copy in ret_copies:
         copy.wait()
     returned = jnp.concatenate([ret_in[0] * lower, ret_in[1] * upper], axis=0)
@@ -297,90 +417,9 @@
         return carry
 
     lax.fori_loop(0, blocks, give_back, 0)
-
-
-def sum_kernel(n_grp, n_dom, part_ref, out_ref, first_in, mine, second_in, send_sem, recv_sem):
-    grp = lax.axis_index("grp")
-    dom = lax.axis_index("dom")
-    plane = n_dom // 2
-    column = n_grp * 2
-    core = lax.rem(dom, 2)
-    place = dom // 2
-    level = grp * 2 + core
-    rows = part_ref.shape[0] // plane
-
-    def in_plane(index):
-        return (grp, index * 2 + core)
-
-    def in_column(index):
-        return (index // 2, place * 2 + lax.rem(index, 2))
-
-    barrier = pltpu.get_barrier_semaphore()
-    for t in range(1, plane):
-        pl.semaphore_signal(
-            barrier, inc=1, device_id=in_plane(lax.rem(place + t, plane)), device_id_type=MESH
-        )
-    for t in range(1, column):
-        pl.semaphore_signal(
-            barrier, inc=1, device_id=in_column(lax.rem(level + t, column)), device_id_type=MESH
-        )
-    pl.semaphore_wait(barrier, plane + column - 2)
-
-    def cut(index):
-        return pl.ds(pl.multiple_of(index * rows, 8), rows)
-
-    def copy(src, dst, index, peer):
-        return pltpu.make_async_remote_copy(
-            src_ref=src,
-            dst_ref=dst,
-            send_sem=send_sem.at[index],
-            recv_sem=recv_sem.at[index],
-            device_id=peer,
-            device_id_type=MESH,
-        )
-
-    def ahead(t):
-        return lax.rem(place + t, plane)
-
-    first = [
-        copy(part_ref.at[cut(ahead(t)), :], first_in.at[place], t, in_plane(ahead(t)))
-        for t in range(1, plane)
-    ]
-    for c in first:
-        c.start()
-    first_in[place] = part_ref[cut(place), :]
-    for c in first:
-        c.wait()
-    total = first_in[0]
-    for t in range(1, plane):
-        total += first_in[t]
-    mine[...] = total
-    second = [
-        copy(mine, second_in.at[level], plane + t, in_column(lax.rem(level + t, column)))
-        for t in range(1, column)
-    ]
-    for c in second:
-        c.start()
-    second_in[level] = total
-    for c in second:
-        c.wait()
-    total = second_in[0]
-    for t in range(1, column):
-        total += second_in[t]
-    out_ref[cut(place), :] = total
-    third = [
-        copy(
-            out_ref.at[cut(place), :],
-            out_ref.at[cut(place), :],
-            plane + column + t,
-            in_plane(ahead(t)),
-        )
-        for t in range(1, plane)
-    ]
-    for c in third:
-        c.start()
-    for c in third:
-        c.wait()
+    sum_b.start_gather()
+    sum_a.finish()
+    sum_b.finish()
 
 
 def finish_kernel(node_ref, sums_ref, out_ref, *rest):
@@ -424,39 +463,8 @@
     block = min(512, fine)
     blocks = fine // block
     vmem = pl.BlockSpec(memory_space=pltpu.VMEM)
-    node_grad, grads = pl.pallas_call(
-        functools.partial(block_kernel, n_dom),
-        out_shape=(
-            jax.ShapeDtypeStruct((fine, width), F32),
-            jax.ShapeDtypeStruct((6 * width, width), F32),
-        ),
-        in_specs=[vmem] * 15,
-        out_specs=(vmem, vmem),
-        scratch_shapes=[
-            pltpu.VMEM((5, sends, width), BF16),
-            pltpu.VMEM((5, sends, width), BF16),
-            pltpu.VMEM((5, sends, width), BF16),
-            pltpu.VMEM((5, sends, width), BF16),
-            pltpu.VMEM((2, rim, width), BF16),
-            pltpu.VMEM((2, rim, width), BF16),
-            pltpu.VMEM((2, rim, width), BF16),
-            pltpu.VMEM((2, rim, width), BF16),
-            pltpu.VMEM((fine, 2 * width), BF16),
-            pltpu.VMEM((fine, width), F32),
-            pltpu.VMEM((block + 2 * rim, 2 * width), BF16),
-            pltpu.VMEM((blocks, slots, block, width), F32),
-            pltpu.VMEM((fine, width), BF16),
-            pltpu.VMEM((128, fine // 128), jnp.int32),
-            pltpu.VMEM((blocks, slots, block), jnp.int32),
-            pltpu.VMEM((2 * rim, width), F32),
-            pltpu.SemaphoreType.DMA((14,)),
-            pltpu.SemaphoreType.DMA((14,)),
-        ],
-        compiler_params=pltpu.CompilerParams(
-            collective_id=0, has_side_effects=True, vmem_limit_bytes=48 * 1024 * 1024
-        ),
-        name="block",
-    )(
+    anywhere = pl.BlockSpec(memory_space=pl.ANY)
+    args = (
         hidden_in,
         cotangent,
         coarse_state,
@@ -473,31 +481,49 @@
         own_slots.reshape(fine // 128, 128),
         coarse_nbrs.T,
     )
-    plane, column = n_dom // 2, n_grp * 2
-    rows = 6 * width // plane
-    sums = pl.pallas_call(
-        functools.partial(sum_kernel, n_grp, n_dom),
-        out_shape=jax.ShapeDtypeStruct((6 * width, width), F32),
-        in_specs=[vmem],
-        out_specs=vmem,
-        scratch_shapes=[
-            pltpu.VMEM((plane, rows, width), F32),
-            pltpu.VMEM((rows, width), F32),
-            pltpu.VMEM((column, rows, width), F32),
-            pltpu.SemaphoreType.DMA((2 * plane + column,)),
-            pltpu.SemaphoreType.DMA((2 * plane + column,)),
+    sum_sems = 2 * (2 * n_dom + n_grp)
+    node_grad, sums = pl.pallas_call(
+        functools.partial(block_kernel, n_grp, n_dom),
+        out_shape=(
+            jax.ShapeDtypeStruct((fine, width), F32),
+            jax.ShapeDtypeStruct((6 * width, width), F32),
+        ),
+        in_specs=[anywhere] * NAMES,
+        out_specs=(vmem, vmem),
+        scratch_shapes=[pltpu.VMEM(a.shape, a.dtype) for a in args]
+        + [pltpu.VMEM((5, sends, width), BF16)] * 4
+        + [pltpu.VMEM((2, rim, width), BF16)] * 4
+        + [
+            pltpu.VMEM((fine, 2 * width), BF16),
+            pltpu.VMEM((fine, width), F32),
+            pltpu.VMEM((block + 2 * rim, 2 * width), BF16),
+            pltpu.VMEM((blocks, slots, block, width), F32),
+            pltpu.VMEM((fine, width), BF16),
+            pltpu.VMEM((blocks, slots, block), jnp.int32),
+            pltpu.VMEM((2 * rim, width), F32),
+            pltpu.VMEM((6 * width, width), F32),
+            pltpu.VMEM((n_dom, 4 * width // n_dom, width), F32),
+            pltpu.VMEM((n_dom, 2 * width // n_dom, width), F32),
+            pltpu.VMEM((4 * width // n_dom, width), F32),
+            pltpu.VMEM((2 * width // n_dom, width), F32),
+            pltpu.VMEM((n_grp, 4 * width // n_dom, width), F32),
+            pltpu.VMEM((n_grp, 2 * width // n_dom, width), F32),
+            pltpu.SemaphoreType.DMA((NAMES,)),
+            pltpu.SemaphoreType.DMA((14,)),
+            pltpu.SemaphoreType.DMA((14,)),
+            pltpu.SemaphoreType.DMA((sum_sems,)),
+            pltpu.SemaphoreType.DMA((sum_sems,)),
         ],
         compiler_params=pltpu.CompilerParams(
-            collective_id=1, has_side_effects=True, vmem_limit_bytes=16 * 1024 * 1024
+            collective_id=0, has_side_effects=True, vmem_limit_bytes=56 * 1024 * 1024
         ),
-        name="sums",
-    )(grads)
-    anywhere = pl.BlockSpec(memory_space=pl.ANY)
+        name="block",
+    )(*args)
     square = jax.ShapeDtypeStruct((width, width), F32)
     return pl.pallas_call(
         finish_kernel,
         out_shape=(jax.ShapeDtypeStruct((fine, width), F32),) + (square,) * 6,
-        in_specs=[anywhere] * 2,
+        in_specs=[vmem] * 2,
         out_specs=(anywhere,) * 7,
         scratch_shapes=[pltpu.SemaphoreType.DMA((7,))],
         name="finish",

time: 131 us -> 66 us (0.50)
  Pallas kernels: 117 us -> 65.2 us
  local copies, waits for them, and re-layouts: 12.8 us -> 0 us
    pallas_call x1, Pallas kernels: 44.8 us -> 2.45 us  [body(): pl.pallas_call(finish_kernel, out_shape=(jax.ShapeDtypeStruct((fine, widt...]
    unnamed x34 -> x0, local copies, waits for them, and re-layouts: 12.8 us -> none
    pallas_call x2 -> x1, Pallas kernels: 72 us -> 62.8 us  [body(): pl.pallas_call(functools.partial(block_kernel, n_grp, n_dom), out_shape=(...]
where the time goes in v2:
time: 66 us; the launch traced here: 65.9 us
  Pallas kernels  65.2 us (99%)
    pallas_call x1, Pallas kernels, body(): pl.pallas_call(functools.partial(block_kernel, n_grp, n_dom), out_shape=(...  62.8 us
    pallas_call x1, Pallas kernels, body(): pl.pallas_call(finish_kernel, out_shape=(jax.ShapeDtypeStruct((fine, widt...  2.45 us

profile of v2, /device:TPU:1, one launch (start us, length us, event | category | flops | bytes accessed | tf_op | source)
XLA Modules:
  0.0 65.9 jit_solution(2252296659290094204)
XLA Ops:
  0.6 62.8 %block.1 = (f32[2048,128]{1,0:T(8,128)}, f32[768,128]{1,0:T(8,128)}) custom-call(bf16[2048,128]{1,0:T(8,128)(2,1)} %refs_0_.1, bf16[2048,128]{1,0:T(8,128)(2,1)} %refs_1_.1, bf16[128,128]{1,0:T(8,128)(2,1)} %refs_2_.1, bf16[128,128]{1,0:T(8,128)(2,1)} %refs_3_.1, bf16[128,128]{1,0:T(8,128)(2,1)} %refs_4_.1, bf16[128,128]{1,0:T(8,128)(2,1)} %refs_5_.1, ...), custom_call_target="tpu_custom_call" | custom-call | tf_op jit(solution)/shard_map/block/pallas_call | solution.py:485
  63.4 2.5 %finish.1 = (f32[2048,128]{1,0:T(8,128)}, f32[128,128]{1,0:T(8,128)}, f32[128,128]{1,0:T(8,128)}, f32[128,128]{1,0:T(8,128)}, f32[128,128]{1,0:T(8,128)}, /*index=5*/f32[128,128]{1,0:T(8,128)}, f32[128,128]{1,0:T(8,128)}) custom-call(f32[2048,128]{1,0:T(8,128)} %get-tuple-element.9.node_ref, f32[768,128]{1,0:T(8,128)} %get-tuple-element.10.sums_ref), custom_call_target="tpu_custom_call" | custom-call | tf_op jit(solution)/shard_map/finish/pallas_call | solution.py:523

commit v3 on v2

--- a/solution.py
+++ b/solution.py
@@ -11,6 +11,7 @@
 F32 = jnp.float32
 BF16 = jnp.bfloat16
 OFF = -1.0e4
+TILE = 256
 
 
 def dot(a, b):
@@ -44,10 +45,11 @@
     return high, (values - high.astype(F32)).astype(BF16)
 
 
-def gate(pre):
-    squash = 0.5 + 0.5 * jnp.tanh(0.5 * pre)
-    act = pre * squash
-    return act, squash + act * (1.0 - squash)
+def gate(half):
+    tilt = jnp.tanh(half)
+    both = 1.0 + tilt
+    act = half * both
+    return act, both + act * (2.0 - both)
 
 
 NAMES = 15
@@ -66,12 +68,13 @@
         rim_in,
         ret_out,
         ret_in,
-        peer_hl,
-        pre_self_ref,
-        window,
+        hots,
+        table_ref,
+        own_half,
         slope_ref,
         pooled_ref,
-        place_ref,
+        up_ref,
+        grad_ref,
         rim_sum,
         part_ref,
         first_a,
@@ -107,10 +110,6 @@
         pltpu.make_async_copy(src, dst, load_sem.at[i])
         for i, (src, dst) in enumerate(zip(inputs, held))
     ]
-    order = (11, 1, 10, 0, 12, 13, 2, 6, 7, 8, 14, 3, 4, 5, 9)
-    for i in order:
-        loads[i].start()
-
     grp = lax.axis_index("grp")
     me = lax.axis_index("dom")
     fine, width = hidden_ref.shape
@@ -120,13 +119,20 @@
     sends = send_ref.shape[1]
     block = min(512, fine)
     blocks = fine // block
-    span = block + 2 * rim
+    halves = block // TILE
+    groups = halves + 2 * rim // TILE
     offsets = (1, -1, 2, -2, n_dom // 2)
     to = [lax.rem(me + (n_dom + o), n_dom) for o in offsets]
     source = [lax.rem(me + (n_dom - o), n_dom) for o in offsets]
 
     barrier = pltpu.get_barrier_semaphore()
 
+    for peer in to:
+        pl.semaphore_signal(barrier, inc=1, device_id=(grp, peer), device_id_type=MESH)
+    order = (11, 1, 10, 0, 12, 13, 2, 6, 7, 8, 14, 3, 4, 5, 9)
+    for i in order:
+        loads[i].start()
+
     def greet_dom(t, carry):
         peer = (grp, lax.rem(me + t, n_dom))
         pl.semaphore_signal(barrier, inc=1, device_id=peer, device_id_type=MESH)
@@ -137,7 +143,8 @@
         pl.semaphore_signal(barrier, inc=1, device_id=peer, device_id_type=MESH)
         return carry
 
-    lax.fori_loop(1, n_dom, greet_dom, 0)
+    lax.fori_loop(3, n_dom // 2, greet_dom, 0)
+    lax.fori_loop(n_dom // 2 + 1, n_dom - 2, greet_dom, 0)
     lax.fori_loop(1, n_grp, greet_grp, 0)
 
     def remote(src, dst, index, peer):
@@ -200,7 +207,7 @@
             self.first[me] = part_ref[self.cut(me), :]
 
         def start_across(self):
-            self.each(self.scatter, n_dom, lambda c: c.wait())
+            self.each(self.scatter, n_dom, lambda c: c.wait_recv())
             total = self.first[0]
             for t in range(1, n_dom):
                 total += self.first[t]
@@ -209,7 +216,7 @@
             self.second[grp] = total
 
         def start_gather(self):
-            self.each(self.across, n_grp, lambda c: c.wait())
+            self.each(self.across, n_grp, lambda c: c.wait_recv())
             total = self.second[0]
             for t in range(1, n_grp):
                 total += self.second[t]
@@ -217,7 +224,10 @@
             self.each(self.gather, n_dom, lambda c: c.start())
 
         def finish(self):
-            self.each(self.gather, n_dom, lambda c: c.wait())
+            self.each(self.gather, n_dom, lambda c: c.wait_recv())
+            self.each(self.scatter, n_dom, lambda c: c.wait_send())
+            self.each(self.across, n_grp, lambda c: c.wait_send())
+            self.each(self.gather, n_dom, lambda c: c.wait_send())
 
     sum_a = Sum(2 * width, 4 * width, first_a, mine_a, second_a, 0)
     sum_b = Sum(0, 2 * width, first_b, mine_b, second_b, 2 * n_dom + n_grp)
@@ -229,34 +239,39 @@
         send_rows + [rim_ref[1:2, :], rim_ref[0:1, :], jnp.zeros((1, sends), jnp.int32)], axis=0
     )
     listed_cols = listed.T
-    for k in range(5):
-        cot_out[k] = dot(in_columns(listed_cols[:, k : k + 1], fine), cot_ref[...]).astype(BF16)
-    pl.semaphore_wait(barrier, n_dom + n_grp - 2)
-    for copy in cot_copies:
-        copy.start()
+    sent = coarse + 5 * sends
+    for step, k in enumerate((4, 2, 3, 0, 1)):
+        hot = in_columns(listed_cols[:, k : k + 1], fine)
+        hots[coarse + k * sends : coarse + (k + 1) * sends, :] = hot
+        cot_out[k] = dot(hot, cot_ref[...]).astype(BF16)
+        if step == 0:
+            pl.semaphore_wait(barrier, n_dom + n_grp - 2)
+        cot_copies[k].start()
     loads[0].wait()
     for k in range(2):
-        rim_out[k] = dot(in_columns(listed_cols[:, 5 + k : 6 + k], fine), hidden_ref[...]).astype(
-            BF16
+        hots[sent + k * rim : sent + (k + 1) * rim, :] = in_columns(
+            listed_cols[:, 5 + k : 6 + k], fine
         )
+    chosen = dot(hots[sent:, :], hidden_ref[...]).astype(BF16)
+    for k in range(2):
+        rim_out[k] = chosen[k * rim : (k + 1) * rim]
     for copy in rim_copies:
         copy.start()
     for i in range(NAMES):
         if i not in (0, 1, 10, 11):
             loads[i].wait()
     member_rows = [member_ref[pl.ds(s, 1), :] for s in source]
-    own_hot = jnp.concatenate(
-        [in_rows(own_ref[t : t + 1, :], coarse) for t in range(fine // 128)], axis=1
+
+    for t in range(fine // 128):
+        hots[0:coarse, t * 128 : (t + 1) * 128] = in_rows(own_ref[t : t + 1, :], coarse)
+    far_hot = jnp.concatenate([in_rows(row, coarse) for row in member_rows], axis=1)
+    own_pull = dot(
+        hots[0:coarse, :], jnp.concatenate([cot_ref[...], jnp.ones((fine, width), BF16)], axis=1)
     )
-    far_hot = jnp.concatenate([in_rows(row, coarse) for row in member_rows], axis=1)
-    own_pull = dot(own_hot, cot_ref[...])
-    members = dot(own_hot, jnp.ones((fine, width), BF16)) + dot(
-        far_hot, jnp.ones((5 * sends, width), BF16)
-    )
 
     coarse_rows = coarse_ref[...]
-    coarse_self = dot(coarse_rows, cws_ref[...])
-    coarse_peer = jnp.concatenate(split(dot(coarse_rows, cwp_ref[...])), axis=1)
+    coarse_self = 0.5 * dot(coarse_rows, cws_ref[...])
+    coarse_peer = jnp.concatenate(split(0.5 * dot(coarse_rows, cwp_ref[...])), axis=1)
     links = cnbrs_ref[...]
     link_cols = links.T
     coarse_slopes = []
@@ -269,151 +284,167 @@
         coarse_pool += act
         coarse_slopes.append(slope)
     coarse_pool = coarse_pool.astype(BF16)
-
-    both = dot(hidden_ref[...], jnp.concatenate([ws_ref[...], wp_ref[...]], axis=1))
-    pre_self_ref[...] = both[:, :width]
-    high, low = split(both[:, width:])
-    peer_hl[0:fine, 0:width] = high
-    peer_hl[0:fine, width:] = low
+    link_hot = jnp.concatenate([in_rows(links[j : j + 1, :], coarse) for j in range(slots)], axis=1)
 
     for copy in cot_copies:
         copy.wait()
-    far_pull = dot(far_hot, cot_in[...].reshape(5 * sends, width))
-    pulled = own_pull + far_pull
+    arrived = cot_in[...].reshape(5 * sends, width)
+    far_pull = dot(
+        far_hot, jnp.concatenate([arrived, jnp.ones((5 * sends, width), BF16)], axis=1)
+    )
+    gathered = own_pull + far_pull
+    pulled = gathered[:, :width]
+    members = gathered[:, width:]
     pulled_b = pulled.astype(BF16)
-    grad_pool = dot_nt(pulled_b, cwo_ref[...])
+    grad_pool = 0.5 * dot_nt(pulled_b, cwo_ref[...])
     grad_sum = jnp.zeros((coarse, width), F32)
-    peer_sum = jnp.zeros((coarse, width), F32)
+    grad_pres = []
     for j in range(slots):
         grad_pre = grad_pool * coarse_slopes[j]
         grad_sum += grad_pre
-        peer_sum += dot(in_rows(links[j : j + 1, :], coarse), grad_pre.astype(BF16))
+        grad_pres.append(grad_pre.astype(BF16))
     grad_sum = grad_sum.astype(BF16)
-    high, low = split(peer_sum)
-    node_grad = pulled + dot_nt(grad_sum, cws_ref[...])
-    node_grad += dot_nt(high, cwp_ref[...]) + dot_nt(low, cwp_ref[...])
-    back = (node_grad / members).astype(BF16)
-    member_cols = jnp.concatenate(
-        member_rows + [jnp.zeros((3, sends), jnp.int32)], axis=0
-    ).T
+    high, low = split(dot(link_hot, jnp.concatenate(grad_pres, axis=0)))
+    node_grad = pulled + dot_nt(
+        jnp.concatenate([grad_sum, high, low], axis=1),
+        jnp.concatenate([cws_ref[...], cwp_ref[...], cwp_ref[...]], axis=1),
+    )
+    back = (node_grad / members).T.astype(BF16)
+    replies = dot(back, far_hot).astype(BF16)
     for k in range(5):
-        rep_out[k] = dot(in_columns(member_cols[:, k : k + 1], coarse), back).astype(BF16)
+        rep_out[k] = replies[:, k * sends : (k + 1) * sends]
     for copy in rep_copies:
         copy.start()
     part_ref[3 * width : 4 * width, :] = dot_tn(coarse_rows, grad_sum)
     part_ref[4 * width : 5 * width, :] = dot_tn(coarse_rows, high) + dot_tn(coarse_rows, low)
     part_ref[5 * width : 6 * width, :] = dot_tn(coarse_pool, pulled_b)
 
+    self_turned = ws_ref[...].T
+    peer_turned = wp_ref[...].T
+    both_turned = jnp.concatenate([self_turned, peer_turned], axis=0)
+    for t in range(fine // TILE):
+        here = slice(t * TILE, (t + 1) * TILE)
+        both = 0.5 * dot_nt(both_turned, hidden_ref[here, :])
+        own_half[:, here] = both[:width]
+        table_ref[t] = both[width:].astype(BF16)
+        up_ref[:, here] = cot_ref[here, :].astype(F32).T
+
     for copy in rim_copies:
         copy.wait()
     lower = jnp.where(me > 0, 1.0, 0.0).astype(BF16)
     upper = jnp.where(me < n_dom - 1, 1.0, 0.0).astype(BF16)
     rims = jnp.concatenate([rim_in[0] * lower, rim_in[1] * upper], axis=0)
-    high, low = split(dot(rims, wp_ref[...]))
-    window[block:, 0:width] = high
-    window[block:, width:] = low
+    for t in range(2 * rim // TILE):
+        here = slice(t * TILE, (t + 1) * TILE)
+        table_ref[fine // TILE + t] = (0.5 * dot_nt(peer_turned, rims[here])).astype(BF16)
+
+    def places(b):
+        first = pl.multiple_of(b * block, block)
+        picked = nbrs_ref[:, pl.ds(first, block)]
+        placed = jnp.where(picked < fine, picked - first, picked - (fine - block))
+        return placed % TILE, placed // TILE
 
     def forward(b, carry):
-        first = pl.multiple_of(b * block, block)
-        here = pl.ds(first, block)
-        picked = nbrs_ref[:, here]
-        placed = jnp.where(picked < fine, picked - first, picked - fine + block)
-        place_ref[b] = placed
-        cols = placed.T
-        window[0:block, :] = peer_hl[here, :]
-        own_pre = pre_self_ref[here, :]
-        total = jnp.zeros((block, width), F32)
+        here = pl.ds(pl.multiple_of(b * block, block), block)
+        near, far = places(b)
+        table = jnp.concatenate(
+            [table_ref[b * halves + t] for t in range(halves)]
+            + [table_ref[fine // TILE + t] for t in range(2 * rim // TILE)],
+            axis=0,
+        )
+        own = own_half[:, here]
+        total = jnp.zeros((width, block), F32)
         for j in range(slots):
-            col = cols[:, j : j + 1]
-            got = dot(in_columns(col, span), window[...])
-            bias = jnp.where(col == span, OFF, 0.0)
-            act, slope = gate(own_pre + got[:, :width] + (got[:, width:] + bias))
+            got = dot(table, in_rows(near[j : j + 1, :], TILE))
+            group = jnp.broadcast_to(far[j : j + 1, :], (width, block))
+            peer = jnp.full((width, block), OFF, F32)
+            for t in range(groups):
+                peer = jnp.where(group == t, got[t * width : (t + 1) * width], peer)
+            act, slope = gate(own + peer)
             total += act
             slope_ref[b, j] = slope
-        pooled_ref[here, :] = total.astype(BF16)
+        pooled_ref[:, here] = total.astype(BF16)
         return carry
 
     lax.fori_loop(0, blocks, forward, 0)
 
     for copy in rep_copies:
         copy.wait()
-    sources = jnp.concatenate([back, rep_in[...].reshape(5 * sends, width)], axis=0)
-    part_ref[0 : 3 * width, :] = jnp.zeros((3 * width, width), F32)
-    rim_sum[...] = jnp.zeros((2 * rim, width), F32)
+    sources = jnp.concatenate([back] + [rep_in[k] for k in range(5)], axis=1)
+
+    def arrive(b, carry):
+        here = pl.ds(pl.multiple_of(b * block, block), block)
+        up_ref[:, here] += dot(sources, hots[0:sent, here])
+        return carry
+
+    lax.fori_loop(0, blocks, arrive, 0)
+    part_ref[2 * width : 3 * width, :] = dot_nt(pooled_ref[...], up_ref[...].astype(BF16))
+    sum_a.start_scatter()
+    rim_sum[...] = jnp.zeros((width, 2 * rim), F32)
     self_weight = ws_ref[...]
     peer_weight = wp_ref[...]
     out_weight = wo_ref[...]
 
-    def arrive(b, carry):
-        first = pl.multiple_of(b * block, block)
-        here = pl.ds(first, block)
-        own_hots = jnp.concatenate(
-            [
-                in_columns(own_ref[pl.ds(b * (block // 128) + t, 1), :].T, coarse)
-                for t in range(block // 128)
-            ],
-            axis=0,
-        )
-        hots = jnp.concatenate([own_hots] + [in_rows(row - first, block) for row in send_rows], axis=1)
-        arriving = cot_ref[here, :].astype(F32) + dot(hots, sources)
-        out_ref[here, :] = arriving
-        part_ref[2 * width : 3 * width, :] += dot_tn(pooled_ref[here, :], arriving.astype(BF16))
-        return carry
-
-    lax.fori_loop(0, blocks, arrive, 0)
-    sum_a.start_scatter()
-
     def backward(b, carry):
         first = pl.multiple_of(b * block, block)
         here = pl.ds(first, block)
-        arriving = out_ref[here, :]
-        grad_pool = dot_nt(arriving.astype(BF16), out_weight)
-        grad_sum = jnp.zeros((block, width), F32)
-        peer_sum = jnp.zeros((span, width), F32)
-        placed = place_ref[b]
+        near, far = places(b)
+        near_cols = near.T
+        grad_pool = 0.5 * dot(out_weight, up_ref[:, here].astype(BF16))
+        grad_sum = jnp.zeros((width, block), F32)
+        peer_sum = jnp.zeros((groups * width, TILE), F32)
         for j in range(slots):
             grad_pre = grad_pool * slope_ref[b, j]
             grad_sum += grad_pre
-            peer_sum += dot(in_rows(placed[j : j + 1, :], span), grad_pre.astype(BF16))
-        grad_sum = grad_sum.astype(BF16)
-        rim_sum[...] += peer_sum[block:]
-        high, low = split(peer_sum[:block])
-        rows = hidden_ref[here, :]
-        got = dot_tn(rows, jnp.concatenate([grad_sum, high, low], axis=1))
-        part_ref[0:width, :] += got[:, :width]
-        part_ref[width : 2 * width, :] += got[:, width : 2 * width] + got[:, 2 * width :]
-        out_ref[here, :] = (
-            arriving
-            + dot_nt(grad_sum, self_weight)
-            + dot_nt(high, peer_weight)
-            + dot_nt(low, peer_weight)
+            grad_b = grad_pre.astype(BF16)
+            group = jnp.broadcast_to(far[j : j + 1, :].astype(jnp.int16), (width, block))
+            zero = jnp.zeros((width, block), BF16)
+            spread = jnp.concatenate(
+                [jnp.where(group == t, grad_b, zero) for t in range(groups)], axis=0
+            )
+            peer_sum += dot(spread, in_columns(near_cols[:, j : j + 1], TILE))
+        grad_ref[0:width, here] = grad_sum.astype(BF16)
+        for t in range(halves):
+            high, low = split(peer_sum[t * width : (t + 1) * width])
+            cut = pl.ds(pl.multiple_of(first + t * TILE, TILE), TILE)
+            grad_ref[width : 2 * width, cut] = high
+            grad_ref[2 * width : 3 * width, cut] = low
+        rim_sum[...] += jnp.concatenate(
+            [peer_sum[t * width : (t + 1) * width] for t in range(halves, groups)], axis=1
         )
         return carry
 
-    half = max(blocks // 2, 1)
-    lax.fori_loop(0, half, backward, 0)
+    lax.fori_loop(0, blocks, backward, 0)
+
+    high, low = split(rim_sum[...])
+    turned = dot(grad_ref[...], hidden_ref[...])
+    peer_grad = turned[width : 2 * width] + turned[2 * width :] + dot(high, rims) + dot(low, rims)
+    part_ref[0:width, :] = turned[:width].T
+    part_ref[width : 2 * width, :] = peer_grad.T
+    sum_b.start_scatter()
     sum_a.start_across()
-    lax.fori_loop(half, blocks, backward, 0)
-    sum_a.start_gather()
-
-    high, low = split(rim_sum[...])
-    part_ref[width : 2 * width, :] += dot_tn(rims, high) + dot_tn(rims, low)
-    sum_b.start_scatter()
-    rim_grad = (dot_nt(high, peer_weight) + dot_nt(low, peer_weight)).astype(BF16)
-    ret_out[0] = rim_grad[rim:]
-    ret_out[1] = rim_grad[:rim]
+    rim_grad = (dot(peer_weight, high) + dot(peer_weight, low)).astype(BF16)
+    ret_out[0] = rim_grad[:, rim:]
+    ret_out[1] = rim_grad[:, :rim]
     for copy in ret_copies:
         copy.start()
+    weights = jnp.concatenate([self_weight, peer_weight, peer_weight], axis=1)
+
+    def own_part(b, carry):
+        here = pl.ds(pl.multiple_of(b * block, block), block)
+        up_ref[:, here] += dot(weights, grad_ref[:, here])
+        return carry
+
+    lax.fori_loop(0, blocks, own_part, 0)
     sum_b.start_across()
+    sum_a.start_gather()
     for copy in ret_copies:
         copy.wait()
-    returned = jnp.concatenate([ret_in[0] * lower, ret_in[1] * upper], axis=0)
+    returned = jnp.concatenate([ret_in[1] * upper, ret_in[0] * lower], axis=1)
 
     def give_back(b, carry):
-        first = pl.multiple_of(b * block, block)
-        here = pl.ds(first, block)
-        hots = jnp.concatenate([in_rows(rim_ref[k : k + 1, :] - first, block) for k in range(2)], axis=1)
-        out_ref[here, :] += dot(hots, returned)
+        here = pl.ds(pl.multiple_of(b * block, block), block)
+        out_ref[here, :] = (up_ref[:, here] + dot(returned, hots[sent:, here])).T
         return carry
 
     lax.fori_loop(0, blocks, give_back, 0)
@@ -494,13 +525,14 @@
         + [pltpu.VMEM((5, sends, width), BF16)] * 4
         + [pltpu.VMEM((2, rim, width), BF16)] * 4
         + [
-            pltpu.VMEM((fine, 2 * width), BF16),
-            pltpu.VMEM((fine, width), F32),
-            pltpu.VMEM((block + 2 * rim, 2 * width), BF16),
-            pltpu.VMEM((blocks, slots, block, width), F32),
-            pltpu.VMEM((fine, width), BF16),
-            pltpu.VMEM((blocks, slots, block), jnp.int32),
-            pltpu.VMEM((2 * rim, width), F32),
+            pltpu.VMEM((coarse + 5 * sends + 2 * rim, fine), BF16),
+            pltpu.VMEM(((fine + 2 * rim) // TILE, width, TILE), BF16),
+            pltpu.VMEM((width, fine), F32),
+            pltpu.VMEM((blocks, slots, width, block), F32),
+            pltpu.VMEM((width, fine), BF16),
+            pltpu.VMEM((width, fine), F32),
+            pltpu.VMEM((3 * width, fine), BF16),
+            pltpu.VMEM((width, 2 * rim), F32),
             pltpu.VMEM((6 * width, width), F32),
             pltpu.VMEM((n_dom, 4 * width // n_dom, width), F32),
             pltpu.VMEM((n_dom, 2 * width // n_dom, width), F32),

time: 66 us -> 54.9 us (0.83)
  Pallas kernels: 65.2 us -> 54.1 us
    pallas_call x1, Pallas kernels: 62.8 us -> 51.7 us  [body(): pl.pallas_call(functools.partial(block_kernel, n_grp, n_dom), out_shape=(...]
where the time goes in v3:
time: 54.9 us; the launch traced here: 54.8 us
  Pallas kernels  54.1 us (99%)
  between operations  0.65 us (1%)
    pallas_call x1, Pallas kernels, body(): pl.pallas_call(functools.partial(block_kernel, n_grp, n_dom), out_shape=(...  51.7 us
    pallas_call x1, Pallas kernels, body(): pl.pallas_call(finish_kernel, out_shape=(jax.ShapeDtypeStruct((fine, widt...  2.45 us

profile of v3, /device:TPU:1, one launch (start us, length us, event | category | flops | bytes accessed | tf_op | source)
XLA Modules:
  0.0 54.8 jit_solution(11496501508041412610)
XLA Ops:
  0.6 51.7 %block.1 = (f32[2048,128]{1,0:T(8,128)}, f32[768,128]{1,0:T(8,128)}) custom-call(bf16[2048,128]{1,0:T(8,128)(2,1)} %refs_0_.1, bf16[2048,128]{1,0:T(8,128)(2,1)} %refs_1_.1, bf16[128,128]{1,0:T(8,128)(2,1)} %refs_2_.1, bf16[128,128]{1,0:T(8,128)(2,1)} %refs_3_.1, bf16[128,128]{1,0:T(8,128)(2,1)} %refs_4_.1, bf16[128,128]{1,0:T(8,128)(2,1)} %refs_5_.1, ...), custom_call_target="tpu_custom_call" | custom-call | tf_op jit(solution)/shard_map/block/pallas_call | solution.py:516
  52.3 2.5 %finish.1 = (f32[2048,128]{1,0:T(8,128)}, f32[128,128]{1,0:T(8,128)}, f32[128,128]{1,0:T(8,128)}, f32[128,128]{1,0:T(8,128)}, f32[128,128]{1,0:T(8,128)}, /*index=5*/f32[128,128]{1,0:T(8,128)}, f32[128,128]{1,0:T(8,128)}) custom-call(f32[2048,128]{1,0:T(8,128)} %get-tuple-element.9.node_ref, f32[768,128]{1,0:T(8,128)} %get-tuple-element.10.sums_ref), custom_call_target="tpu_custom_call" | custom-call | tf_op jit(solution)/shard_map/finish/pallas_call | solution.py:555

commit v4 on v3

--- a/solution.py
+++ b/solution.py
@@ -166,73 +166,79 @@
         def __init__(self, base, size, first, mine, second, sems):
             self.base, self.rows = base, size // n_dom
             self.first, self.mine, self.second, self.sems = first, mine, second, sems
-
-        def copy(self, src, dst, index, peer):
+            self.stages = (
+                first.at[pl.ds(0, n_dom - 1)],
+                second.at[pl.ds(0, n_grp - 1)],
+                grads_ref.at[pl.ds(base, (n_dom - 1) * self.rows), :],
+            )
+
+        def copy(self, src, dst, stage, peer):
             return pltpu.make_async_remote_copy(
                 src_ref=src,
                 dst_ref=dst,
-                send_sem=sum_send.at[self.sems + index],
-                recv_sem=sum_recv.at[self.sems + index],
+                send_sem=sum_send.at[self.sems + stage],
+                recv_sem=sum_recv.at[self.sems + stage],
                 device_id=peer,
                 device_id_type=MESH,
             )
 
+        def wait(self, sems, stage):
+            whole = self.stages[stage]
+            pltpu.make_async_copy(whole, whole, sems.at[self.sems + stage]).wait()
+
         def cut(self, index):
             return pl.ds(pl.multiple_of(self.base + index * self.rows, 8), self.rows)
 
-        def scatter(self, t):
-            peer = lax.rem(me + t, n_dom)
-            return self.copy(
-                part_ref.at[self.cut(peer), :], self.first.at[me], t, (grp, peer)
-            )
-
-        def across(self, t):
-            peer = lax.rem(grp + t, n_grp)
-            return self.copy(self.mine, self.second.at[grp], n_dom + t, (peer, me))
-
-        def gather(self, t):
-            peer = lax.rem(me + t, n_dom)
-            mine = grads_ref.at[self.cut(me), :]
-            return self.copy(mine, mine, n_dom + n_grp + t, (grp, peer))
-
-        def each(self, make, count, act):
+        def start_scatter(self):
             def step(t, carry):
-                act(make(t))
+                peer = lax.rem(me + t, n_dom)
+                self.copy(
+                    part_ref.at[self.cut(peer), :], self.first.at[me], 0, (grp, peer)
+                ).start()
                 return carry
 
-            lax.fori_loop(1, count, step, 0)
-
-        def start_scatter(self):
-            self.each(self.scatter, n_dom, lambda c: c.start())
+            lax.fori_loop(1, n_dom, step, 0)
             self.first[me] = part_ref[self.cut(me), :]
 
         def start_across(self):
-            self.each(self.scatter, n_dom, lambda c: c.wait_recv())
+            self.wait(sum_recv, 0)
             total = self.first[0]
             for t in range(1, n_dom):
                 total += self.first[t]
             self.mine[...] = total
-            self.each(self.across, n_grp, lambda c: c.start())
+
+            def step(t, carry):
+                peer = lax.rem(grp + t, n_grp)
+                self.copy(self.mine, self.second.at[grp], 1, (peer, me)).start()
+                return carry
+
+            lax.fori_loop(1, n_grp, step, 0)
             self.second[grp] = total
 
         def start_gather(self):
-            self.each(self.across, n_grp, lambda c: c.wait_recv())
+            self.wait(sum_recv, 1)
             total = self.second[0]
             for t in range(1, n_grp):
                 total += self.second[t]
             grads_ref[self.cut(me), :] = total
-            self.each(self.gather, n_dom, lambda c: c.start())
+            mine = grads_ref.at[self.cut(me), :]
+
+            def step(t, carry):
+                peer = lax.rem(me + t, n_dom)
+                self.copy(mine, mine, 2, (grp, peer)).start()
+                return carry
+
+            lax.fori_loop(1, n_dom, step, 0)
 
         def finish(self):
-            self.each(self.gather, n_dom, lambda c: c.wait_recv())
-            self.each(self.scatter, n_dom, lambda c: c.wait_send())
-            self.each(self.across, n_grp, lambda c: c.wait_send())
-            self.each(self.gather, n_dom, lambda c: c.wait_send())
+            for stage in range(3):
+                self.wait(sum_send, stage)
+            self.wait(sum_recv, 2)
 
     sum_a = Sum(2 * width, 4 * width, first_a, mine_a, second_a, 0)
-    sum_b = Sum(0, 2 * width, first_b, mine_b, second_b, 2 * n_dom + n_grp)
-
-    for i in (11, 10, 1):
+    sum_b = Sum(0, 2 * width, first_b, mine_b, second_b, 3)
+
+    for i in (11, 10):
         loads[i].wait()
     send_rows = [send_ref[pl.ds(t, 1), :] for t in to]
     listed = jnp.concatenate(
@@ -240,12 +246,17 @@
     )
     listed_cols = listed.T
     sent = coarse + 5 * sends
-    for step, k in enumerate((4, 2, 3, 0, 1)):
-        hot = in_columns(listed_cols[:, k : k + 1], fine)
-        hots[coarse + k * sends : coarse + (k + 1) * sends, :] = hot
-        cot_out[k] = dot(hot, cot_ref[...]).astype(BF16)
-        if step == 0:
-            pl.semaphore_wait(barrier, n_dom + n_grp - 2)
+    for k in range(5):
+        hots[coarse + k * sends : coarse + (k + 1) * sends, :] = in_columns(
+            listed_cols[:, k : k + 1], fine
+        )
+    loads[1].wait()
+    for k in range(5):
+        cot_out[k] = dot(
+            hots[coarse + k * sends : coarse + (k + 1) * sends, :], cot_ref[...]
+        ).astype(BF16)
+    pl.semaphore_wait(barrier, n_dom + n_grp - 2)
+    for k in (4, 2, 3, 0, 1):
         cot_copies[k].start()
     loads[0].wait()
     for k in range(2):
@@ -512,7 +523,6 @@
         own_slots.reshape(fine // 128, 128),
         coarse_nbrs.T,
     )
-    sum_sems = 2 * (2 * n_dom + n_grp)
     node_grad, sums = pl.pallas_call(
         functools.partial(block_kernel, n_grp, n_dom),
         out_shape=(
@@ -543,8 +553,8 @@
             pltpu.SemaphoreType.DMA((NAMES,)),
             pltpu.SemaphoreType.DMA((14,)),
             pltpu.SemaphoreType.DMA((14,)),
-            pltpu.SemaphoreType.DMA((sum_sems,)),
-            pltpu.SemaphoreType.DMA((sum_sems,)),
+            pltpu.SemaphoreType.DMA((6,)),
+            pltpu.SemaphoreType.DMA((6,)),
         ],
         compiler_params=pltpu.CompilerParams(
             collective_id=0, has_side_effects=True, vmem_limit_bytes=56 * 1024 * 1024

time: 54.9 us -> 51.5 us (0.938)
  Pallas kernels: 54.1 us -> 50.7 us
    pallas_call x1, Pallas kernels: 51.7 us -> 48.2 us  [body(): pl.pallas_call(functools.partial(block_kernel, n_grp, n_dom), out_shape=(...]
where the time goes in v4:
time: 51.5 us; the launch traced here: 51.3 us
  Pallas kernels  50.7 us (98%)
  between operations  0.65 us (1%)
    pallas_call x1, Pallas kernels, body(): pl.pallas_call(functools.partial(block_kernel, n_grp, n_dom), out_shape=(...  48.2 us
    pallas_call x1, Pallas kernels, body(): pl.pallas_call(finish_kernel, out_shape=(jax.ShapeDtypeStruct((fine, widt...  2.45 us

profile of v4, /device:TPU:1, one launch (start us, length us, event | category | flops | bytes accessed | tf_op | source)
XLA Modules:
  0.0 51.3 jit_solution(9317460056948085953)
XLA Ops:
  0.6 48.2 %block.1 = (f32[2048,128]{1,0:T(8,128)}, f32[768,128]{1,0:T(8,128)}) custom-call(bf16[2048,128]{1,0:T(8,128)(2,1)} %refs_0_.1, bf16[2048,128]{1,0:T(8,128)(2,1)} %refs_1_.1, bf16[128,128]{1,0:T(8,128)(2,1)} %refs_2_.1, bf16[128,128]{1,0:T(8,128)(2,1)} %refs_3_.1, bf16[128,128]{1,0:T(8,128)(2,1)} %refs_4_.1, bf16[128,128]{1,0:T(8,128)(2,1)} %refs_5_.1, ...), custom_call_target="tpu_custom_call" | custom-call | tf_op jit(solution)/shard_map/block/pallas_call | solution.py:526
  48.8 2.5 %finish.1 = (f32[2048,128]{1,0:T(8,128)}, f32[128,128]{1,0:T(8,128)}, f32[128,128]{1,0:T(8,128)}, f32[128,128]{1,0:T(8,128)}, f32[128,128]{1,0:T(8,128)}, /*index=5*/f32[128,128]{1,0:T(8,128)}, f32[128,128]{1,0:T(8,128)}) custom-call(f32[2048,128]{1,0:T(8,128)} %get-tuple-element.9.node_ref, f32[768,128]{1,0:T(8,128)} %get-tuple-element.10.sums_ref), custom_call_target="tpu_custom_call" | custom-call | tf_op jit(solution)/shard_map/finish/pallas_call | solution.py:565

commit v5 on v4

--- a/solution.py
+++ b/solution.py
@@ -83,11 +83,15 @@
         mine_b,
         second_a,
         second_b,
+        done_a,
+        done_b,
+        turned_out,
         load_sem,
         send_sem,
         recv_sem,
         sum_send,
         sum_recv,
+        write_sem,
     ) = refs[2 * NAMES + 2 :]
     (
         hidden_ref,
@@ -143,9 +147,9 @@
         pl.semaphore_signal(barrier, inc=1, device_id=peer, device_id_type=MESH)
         return carry
 
-    lax.fori_loop(3, n_dom // 2, greet_dom, 0)
-    lax.fori_loop(n_dom // 2 + 1, n_dom - 2, greet_dom, 0)
-    lax.fori_loop(1, n_grp, greet_grp, 0)
+    lax.fori_loop(3, n_dom // 2, greet_dom, 0, unroll=True)
+    lax.fori_loop(n_dom // 2 + 1, n_dom - 2, greet_dom, 0, unroll=True)
+    lax.fori_loop(1, n_grp, greet_grp, 0, unroll=True)
 
     def remote(src, dst, index, peer):
         return pltpu.make_async_remote_copy(
@@ -162,10 +166,22 @@
     rep_copies = [remote(rep_out.at[k], rep_in.at[k], 7 + k, source[k]) for k in range(5)]
     ret_copies = [remote(ret_out.at[k], ret_in.at[k], 12 + k, to[k]) for k in range(2)]
 
+    def hops(t):
+        along_y = n_dom // 4
+        x, y = t / along_y, (t % along_y) / 2
+        return min(x, 4 - x) + min(y, along_y / 2 - y)
+
+    dom_order = sorted(range(1, n_dom), key=hops, reverse=True)
+    grp_order = sorted(range(1, n_grp), key=lambda t: -min(t, n_grp - t))
+
     class Sum:
-        def __init__(self, base, size, first, mine, second, sems):
+        def __init__(self, base, size, first, mine, second, done, sems):
             self.base, self.rows = base, size // n_dom
-            self.first, self.mine, self.second, self.sems = first, mine, second, sems
+            self.first, self.mine, self.second = first, mine, second
+            self.done, self.sems = done, sems
+            self.keep = pltpu.make_async_copy(
+                done, grads_ref.at[self.cut(me), :], write_sem.at[sems // 3]
+            )
             self.stages = (
                 first.at[pl.ds(0, n_dom - 1)],
                 second.at[pl.ds(0, n_grp - 1)],
@@ -190,14 +206,11 @@
             return pl.ds(pl.multiple_of(self.base + index * self.rows, 8), self.rows)
 
         def start_scatter(self):
-            def step(t, carry):
+            for t in dom_order:
                 peer = lax.rem(me + t, n_dom)
                 self.copy(
                     part_ref.at[self.cut(peer), :], self.first.at[me], 0, (grp, peer)
                 ).start()
-                return carry
-
-            lax.fori_loop(1, n_dom, step, 0)
             self.first[me] = part_ref[self.cut(me), :]
 
         def start_across(self):
@@ -206,13 +219,9 @@
             for t in range(1, n_dom):
                 total += self.first[t]
             self.mine[...] = total
-
-            def step(t, carry):
+            for t in grp_order:
                 peer = lax.rem(grp + t, n_grp)
                 self.copy(self.mine, self.second.at[grp], 1, (peer, me)).start()
-                return carry
-
-            lax.fori_loop(1, n_grp, step, 0)
             self.second[grp] = total
 
         def start_gather(self):
@@ -220,23 +229,21 @@
             total = self.second[0]
             for t in range(1, n_grp):
                 total += self.second[t]
-            grads_ref[self.cut(me), :] = total
-            mine = grads_ref.at[self.cut(me), :]
-
-            def step(t, carry):
+            self.done[...] = total
+            place = grads_ref.at[self.cut(me), :]
+            for t in dom_order:
                 peer = lax.rem(me + t, n_dom)
-                self.copy(mine, mine, 2, (grp, peer)).start()
-                return carry
-
-            lax.fori_loop(1, n_dom, step, 0)
+                self.copy(self.done, place, 2, (grp, peer)).start()
+            self.keep.start()
 
         def finish(self):
             for stage in range(3):
                 self.wait(sum_send, stage)
             self.wait(sum_recv, 2)
-
-    sum_a = Sum(2 * width, 4 * width, first_a, mine_a, second_a, 0)
-    sum_b = Sum(0, 2 * width, first_b, mine_b, second_b, 3)
+            self.keep.wait()
+
+    sum_a = Sum(2 * width, 4 * width, first_a, mine_a, second_a, done_a, 0)
+    sum_b = Sum(0, 2 * width, first_b, mine_b, second_b, done_b, 3)
 
     for i in (11, 10):
         loads[i].wait()
@@ -276,9 +283,14 @@
     for t in range(fine // 128):
         hots[0:coarse, t * 128 : (t + 1) * 128] = in_rows(own_ref[t : t + 1, :], coarse)
     far_hot = jnp.concatenate([in_rows(row, coarse) for row in member_rows], axis=1)
-    own_pull = dot(
-        hots[0:coarse, :], jnp.concatenate([cot_ref[...], jnp.ones((fine, width), BF16)], axis=1)
+    own_pull = dot(hots[0:coarse, :], cot_ref[...])
+    members = dot(hots[0:coarse, :], jnp.ones((fine, width), BF16)) + dot(
+        far_hot, jnp.ones((5 * sends, width), BF16)
     )
+    share = 1.0 / members
+    out_turned = (0.5 * cwo_ref[...].astype(F32)).T.astype(BF16)
+    peer_turned = cwp_ref[...].T
+    all_turned = jnp.concatenate([cws_ref[...].T, peer_turned, peer_turned], axis=0)
 
     coarse_rows = coarse_ref[...]
     coarse_self = 0.5 * dot(coarse_rows, cws_ref[...])
@@ -298,16 +310,11 @@
     link_hot = jnp.concatenate([in_rows(links[j : j + 1, :], coarse) for j in range(slots)], axis=1)
 
     for copy in cot_copies:
-        copy.wait()
+        copy.wait_recv()
     arrived = cot_in[...].reshape(5 * sends, width)
-    far_pull = dot(
-        far_hot, jnp.concatenate([arrived, jnp.ones((5 * sends, width), BF16)], axis=1)
-    )
-    gathered = own_pull + far_pull
-    pulled = gathered[:, :width]
-    members = gathered[:, width:]
+    pulled = own_pull + dot(far_hot, arrived)
     pulled_b = pulled.astype(BF16)
-    grad_pool = 0.5 * dot_nt(pulled_b, cwo_ref[...])
+    grad_pool = dot(pulled_b, out_turned)
     grad_sum = jnp.zeros((coarse, width), F32)
     grad_pres = []
     for j in range(slots):
@@ -316,11 +323,8 @@
         grad_pres.append(grad_pre.astype(BF16))
     grad_sum = grad_sum.astype(BF16)
     high, low = split(dot(link_hot, jnp.concatenate(grad_pres, axis=0)))
-    node_grad = pulled + dot_nt(
-        jnp.concatenate([grad_sum, high, low], axis=1),
-        jnp.concatenate([cws_ref[...], cwp_ref[...], cwp_ref[...]], axis=1),
-    )
-    back = (node_grad / members).T.astype(BF16)
+    node_grad = pulled + dot(jnp.concatenate([grad_sum, high, low], axis=1), all_turned)
+    back = (node_grad * share).T.astype(BF16)
     replies = dot(back, far_hot).astype(BF16)
     for k in range(5):
         rep_out[k] = replies[:, k * sends : (k + 1) * sends]
@@ -341,7 +345,7 @@
         up_ref[:, here] = cot_ref[here, :].astype(F32).T
 
     for copy in rim_copies:
-        copy.wait()
+        copy.wait_recv()
     lower = jnp.where(me > 0, 1.0, 0.0).astype(BF16)
     upper = jnp.where(me < n_dom - 1, 1.0, 0.0).astype(BF16)
     rims = jnp.concatenate([rim_in[0] * lower, rim_in[1] * upper], axis=0)
@@ -380,7 +384,7 @@
     lax.fori_loop(0, blocks, forward, 0)
 
     for copy in rep_copies:
-        copy.wait()
+        copy.wait_recv()
     sources = jnp.concatenate([back] + [rep_in[k] for k in range(5)], axis=1)
 
     def arrive(b, carry):
@@ -402,19 +406,26 @@
         near, far = places(b)
         near_cols = near.T
         grad_pool = 0.5 * dot(out_weight, up_ref[:, here].astype(BF16))
-        grad_sum = jnp.zeros((width, block), F32)
         peer_sum = jnp.zeros((groups * width, TILE), F32)
-        for j in range(slots):
-            grad_pre = grad_pool * slope_ref[b, j]
-            grad_sum += grad_pre
-            grad_b = grad_pre.astype(BF16)
-            group = jnp.broadcast_to(far[j : j + 1, :].astype(jnp.int16), (width, block))
-            zero = jnp.zeros((width, block), BF16)
-            spread = jnp.concatenate(
-                [jnp.where(group == t, grad_b, zero) for t in range(groups)], axis=0
-            )
-            peer_sum += dot(spread, in_columns(near_cols[:, j : j + 1], TILE))
-        grad_ref[0:width, here] = grad_sum.astype(BF16)
+        for c in range(block // TILE):
+            lo = c * TILE
+            total = jnp.zeros((width, TILE), F32)
+            left, right = [], []
+            for j in range(slots):
+                grad_pre = grad_pool[:, lo : lo + TILE] * slope_ref[b, j, :, lo : lo + TILE]
+                total += grad_pre
+                grad_b = grad_pre.astype(BF16)
+                group = jnp.broadcast_to(
+                    far[j : j + 1, lo : lo + TILE].astype(jnp.int16), (width, TILE)
+                )
+                zero = jnp.zeros((width, TILE), BF16)
+                left.append(
+                    jnp.concatenate([jnp.where(group == t, grad_b, zero) for t in range(groups)], axis=0)
+                )
+                right.append(in_columns(near_cols[lo : lo + TILE, j : j + 1], TILE))
+            peer_sum += dot(jnp.concatenate(left, axis=1), jnp.concatenate(right, axis=0))
+            cut = pl.ds(pl.multiple_of(first + lo, TILE), TILE)
+            grad_ref[0:width, cut] = total.astype(BF16)
         for t in range(halves):
             high, low = split(peer_sum[t * width : (t + 1) * width])
             cut = pl.ds(pl.multiple_of(first + t * TILE, TILE), TILE)
@@ -449,17 +460,28 @@
     lax.fori_loop(0, blocks, own_part, 0)
     sum_b.start_across()
     sum_a.start_gather()
+    sum_b.start_gather()
     for copy in ret_copies:
-        copy.wait()
+        copy.wait_recv()
     returned = jnp.concatenate([ret_in[1] * upper, ret_in[0] * lower], axis=1)
 
     def give_back(b, carry):
         here = pl.ds(pl.multiple_of(b * block, block), block)
-        out_ref[here, :] = (up_ref[:, here] + dot(returned, hots[sent:, here])).T
+        turned_out[here, :] = (up_ref[:, here] + dot(returned, hots[sent:, here])).T
+        write(b).start()
         return carry
 
+    def write(b):
+        here = pl.ds(pl.multiple_of(b * block, block), block)
+        return pltpu.make_async_copy(
+            turned_out.at[here, :], out_ref.at[here, :], write_sem.at[2 + b]
+        )
+
     lax.fori_loop(0, blocks, give_back, 0)
-    sum_b.start_gather()
+    for copy in cot_copies + rim_copies + rep_copies + ret_copies:
+        copy.wait_send()
+    for b in range(blocks):
+        write(b).wait()
     sum_a.finish()
     sum_b.finish()
 
@@ -530,7 +552,7 @@
             jax.ShapeDtypeStruct((6 * width, width), F32),
         ),
         in_specs=[anywhere] * NAMES,
-        out_specs=(vmem, vmem),
+        out_specs=(anywhere, anywhere),
         scratch_shapes=[pltpu.VMEM(a.shape, a.dtype) for a in args]
         + [pltpu.VMEM((5, sends, width), BF16)] * 4
         + [pltpu.VMEM((2, rim, width), BF16)] * 4
@@ -550,11 +572,15 @@
             pltpu.VMEM((2 * width // n_dom, width), F32),
             pltpu.VMEM((n_grp, 4 * width // n_dom, width), F32),
             pltpu.VMEM((n_grp, 2 * width // n_dom, width), F32),
+            pltpu.VMEM((4 * width // n_dom, width), F32),
+            pltpu.VMEM((2 * width // n_dom, width), F32),
+            pltpu.VMEM((fine, width), F32),
             pltpu.SemaphoreType.DMA((NAMES,)),
             pltpu.SemaphoreType.DMA((14,)),
             pltpu.SemaphoreType.DMA((14,)),
             pltpu.SemaphoreType.DMA((6,)),
             pltpu.SemaphoreType.DMA((6,)),
+            pltpu.SemaphoreType.DMA((2 + blocks,)),
         ],
         compiler_params=pltpu.CompilerParams(
             collective_id=0, has_side_effects=True, vmem_limit_bytes=56 * 1024 * 1024

time: 51.5 us -> 48.4 us (0.940)
  Pallas kernels: 50.7 us -> 47.6 us
    pallas_call x1, Pallas kernels: 48.2 us -> 45.2 us  [body(): pl.pallas_call(functools.partial(block_kernel, n_grp, n_dom), out_shape=(...]
where the time goes in v5:
time: 48.4 us; the launch traced here: 48.3 us
  Pallas kernels  47.6 us (98%)
  between operations  0.65 us (1%)
    pallas_call x1, Pallas kernels, body(): pl.pallas_call(functools.partial(block_kernel, n_grp, n_dom), out_shape=(...  45.2 us
    pallas_call x1, Pallas kernels, body(): pl.pallas_call(finish_kernel, out_shape=(jax.ShapeDtypeStruct((fine, widt...  2.45 us

profile of v5, /device:TPU:1, one launch (start us, length us, event | category | flops | bytes accessed | tf_op | source)
XLA Modules:
  0.0 48.3 jit_solution(16281119626998410346)
XLA Ops:
  0.6 45.2 %block.1 = (f32[2048,128]{1,0:T(8,128)}, f32[768,128]{1,0:T(8,128)}) custom-call(bf16[2048,128]{1,0:T(8,128)(2,1)} %refs_0_.1, bf16[2048,128]{1,0:T(8,128)(2,1)} %refs_1_.1, bf16[128,128]{1,0:T(8,128)(2,1)} %refs_2_.1, bf16[128,128]{1,0:T(8,128)(2,1)} %refs_3_.1, bf16[128,128]{1,0:T(8,128)(2,1)} %refs_4_.1, bf16[128,128]{1,0:T(8,128)(2,1)} %refs_5_.1, ...), custom_call_target="tpu_custom_call" | custom-call | tf_op jit(solution)/shard_map/block/pallas_call | solution.py:548
  45.8 2.5 %finish.1 = (f32[2048,128]{1,0:T(8,128)}, f32[128,128]{1,0:T(8,128)}, f32[128,128]{1,0:T(8,128)}, f32[128,128]{1,0:T(8,128)}, f32[128,128]{1,0:T(8,128)}, /*index=5*/f32[128,128]{1,0:T(8,128)}, f32[128,128]{1,0:T(8,128)}) custom-call(f32[2048,128]{1,0:T(8,128)} %get-tuple-element.9.node_ref, f32[768,128]{1,0:T(8,128)} %get-tuple-element.10.sums_ref), custom_call_target="tpu_custom_call" | custom-call | tf_op jit(solution)/shard_map/finish/pallas_call | solution.py:591

commit v6 on v5

--- a/solution.py
+++ b/solution.py
@@ -12,6 +12,7 @@
 BF16 = jnp.bfloat16
 OFF = -1.0e4
 TILE = 256
+CUTS = 4
 
 
 def dot(a, b):
@@ -309,6 +310,16 @@
     coarse_pool = coarse_pool.astype(BF16)
     link_hot = jnp.concatenate([in_rows(links[j : j + 1, :], coarse) for j in range(slots)], axis=1)
 
+    self_turned = ws_ref[...].T
+    peer_turned = wp_ref[...].T
+    both_turned = jnp.concatenate([self_turned, peer_turned], axis=0)
+    for t in range(fine // TILE):
+        here = slice(t * TILE, (t + 1) * TILE)
+        both = 0.5 * dot_nt(both_turned, hidden_ref[here, :])
+        own_half[:, here] = both[:width]
+        table_ref[t] = both[width:].astype(BF16)
+        up_ref[:, here] = cot_ref[here, :].astype(F32).T
+
     for copy in cot_copies:
         copy.wait_recv()
     arrived = cot_in[...].reshape(5 * sends, width)
@@ -333,16 +344,6 @@
     part_ref[3 * width : 4 * width, :] = dot_tn(coarse_rows, grad_sum)
     part_ref[4 * width : 5 * width, :] = dot_tn(coarse_rows, high) + dot_tn(coarse_rows, low)
     part_ref[5 * width : 6 * width, :] = dot_tn(coarse_pool, pulled_b)
-
-    self_turned = ws_ref[...].T
-    peer_turned = wp_ref[...].T
-    both_turned = jnp.concatenate([self_turned, peer_turned], axis=0)
-    for t in range(fine // TILE):
-        here = slice(t * TILE, (t + 1) * TILE)
-        both = 0.5 * dot_nt(both_turned, hidden_ref[here, :])
-        own_half[:, here] = both[:width]
-        table_ref[t] = both[width:].astype(BF16)
-        up_ref[:, here] = cot_ref[here, :].astype(F32).T
 
     for copy in rim_copies:
         copy.wait_recv()
@@ -487,17 +488,29 @@
 
 
 def finish_kernel(node_ref, sums_ref, out_ref, *rest):
-    parts, sem = rest[:-1], rest[-1]
+    parts, (node_held, sums_held, load_sem, sem) = rest[:6], rest[6:]
     width = sums_ref.shape[1]
-    copies = [pltpu.make_async_copy(node_ref, out_ref, sem.at[6])]
+    size = node_ref.shape[0] // CUTS
+    moves = []
+    for t in range(CUTS):
+        here = pl.ds(t * size, size)
+        moves.append((node_ref.at[here, :], node_held.at[here, :], out_ref.at[here, :]))
     for k, part in enumerate(parts):
-        copies.append(
-            pltpu.make_async_copy(sums_ref.at[pl.ds(k * width, width), :], part, sem.at[k])
-        )
-    for copy in copies:
-        copy.start()
-    for copy in copies:
-        copy.wait()
+        here = pl.ds(k * width, width)
+        moves.append((sums_ref.at[here, :], sums_held.at[here, :], part))
+    loads = [
+        pltpu.make_async_copy(src, held, load_sem.at[i]) for i, (src, held, _) in enumerate(moves)
+    ]
+    writes = [
+        pltpu.make_async_copy(held, dst, sem.at[i]) for i, (_, held, dst) in enumerate(moves)
+    ]
+    for load in loads:
+        load.start()
+    for load, write in zip(loads, writes):
+        load.wait()
+        write.start()
+    for write in writes:
+        write.wait()
 
 
 def body(
@@ -591,9 +604,15 @@
     return pl.pallas_call(
         finish_kernel,
         out_shape=(jax.ShapeDtypeStruct((fine, width), F32),) + (square,) * 6,
-        in_specs=[vmem] * 2,
+        in_specs=[anywhere] * 2,
         out_specs=(anywhere,) * 7,
-        scratch_shapes=[pltpu.SemaphoreType.DMA((7,))],
+        scratch_shapes=[
+            pltpu.VMEM((fine, width), F32),
+            pltpu.VMEM((6 * width, width), F32),
+            pltpu.SemaphoreType.DMA((6 + CUTS,)),
+            pltpu.SemaphoreType.DMA((6 + CUTS,)),
+        ],
+        compiler_params=pltpu.CompilerParams(vmem_limit_bytes=56 * 1024 * 1024),
         name="finish",
     )(node_grad, sums)
 

time: 48.4 us -> 48.2 us (level)
  no operation moved by 1% of the time
where the time goes in v6:
time: 48.2 us; the launch traced here: 48 us
  Pallas kernels  47.4 us (98%)
  between operations  0.65 us (1%)
    pallas_call x1, Pallas kernels, body(): pl.pallas_call(functools.partial(block_kernel, n_grp, n_dom), out_shape=(...  45.1 us
    pallas_call x1, Pallas kernels, body(): pl.pallas_call(finish_kernel, out_shape=(jax.ShapeDtypeStruct((fine, widt...  2.21 us

profile of v6, /device:TPU:1, one launch (start us, length us, event | category | flops | bytes accessed | tf_op | source)
XLA Modules:
  0.0 48.0 jit_solution(4258771855756060710)
XLA Ops:
  0.6 45.1 %block.1 = (f32[2048,128]{1,0:T(8,128)}, f32[768,128]{1,0:T(8,128)}) custom-call(bf16[2048,128]{1,0:T(8,128)(2,1)} %refs_0_.1, bf16[2048,128]{1,0:T(8,128)(2,1)} %refs_1_.1, bf16[128,128]{1,0:T(8,128)(2,1)} %refs_2_.1, bf16[128,128]{1,0:T(8,128)(2,1)} %refs_3_.1, bf16[128,128]{1,0:T(8,128)(2,1)} %refs_4_.1, bf16[128,128]{1,0:T(8,128)(2,1)} %refs_5_.1, ...), custom_call_target="tpu_custom_call" | custom-call | tf_op jit(solution)/shard_map/block/pallas_call | solution.py:561
  45.8 2.2 %finish.1 = (f32[2048,128]{1,0:T(8,128)}, f32[128,128]{1,0:T(8,128)}, f32[128,128]{1,0:T(8,128)}, f32[128,128]{1,0:T(8,128)}, f32[128,128]{1,0:T(8,128)}, /*index=5*/f32[128,128]{1,0:T(8,128)}, f32[128,128]{1,0:T(8,128)}) custom-call(f32[2048,128]{1,0:T(8,128)} %get-tuple-element.9.node_ref, f32[768,128]{1,0:T(8,128)} %get-tuple-element.10.sums_ref), custom_call_target="tpu_custom_call" | custom-call | tf_op jit(solution)/shard_map/finish/pallas_call | solution.py:604

commit v7 on v6

--- a/solution.py
+++ b/solution.py
@@ -378,7 +378,7 @@
                 peer = jnp.where(group == t, got[t * width : (t + 1) * width], peer)
             act, slope = gate(own + peer)
             total += act
-            slope_ref[b, j] = slope
+            slope_ref[b, j] = slope.astype(BF16)
         pooled_ref[:, here] = total.astype(BF16)
         return carry
 
@@ -406,16 +406,15 @@
         here = pl.ds(first, block)
         near, far = places(b)
         near_cols = near.T
-        grad_pool = 0.5 * dot(out_weight, up_ref[:, here].astype(BF16))
+        grad_pool = (0.5 * dot(out_weight, up_ref[:, here].astype(BF16))).astype(BF16)
         peer_sum = jnp.zeros((groups * width, TILE), F32)
         for c in range(block // TILE):
             lo = c * TILE
             total = jnp.zeros((width, TILE), F32)
             left, right = [], []
             for j in range(slots):
-                grad_pre = grad_pool[:, lo : lo + TILE] * slope_ref[b, j, :, lo : lo + TILE]
-                total += grad_pre
-                grad_b = grad_pre.astype(BF16)
+                grad_b = grad_pool[:, lo : lo + TILE] * slope_ref[b, j, :, lo : lo + TILE]
+                total += grad_b.astype(F32)
                 group = jnp.broadcast_to(
                     far[j : j + 1, lo : lo + TILE].astype(jnp.int16), (width, TILE)
                 )
@@ -573,7 +572,7 @@
             pltpu.VMEM((coarse + 5 * sends + 2 * rim, fine), BF16),
             pltpu.VMEM(((fine + 2 * rim) // TILE, width, TILE), BF16),
             pltpu.VMEM((width, fine), F32),
-            pltpu.VMEM((blocks, slots, width, block), F32),
+            pltpu.VMEM((blocks, slots, width, block), BF16),
             pltpu.VMEM((width, fine), BF16),
             pltpu.VMEM((width, fine), F32),
             pltpu.VMEM((3 * width, fine), BF16),

time: 48.2 us -> 47.9 us (level)
  no operation moved by 1% of the time
where the time goes in v7:
time: 47.9 us; the launch traced here: 47.7 us
  Pallas kernels  47.1 us (98%)
  between operations  0.65 us (1%)
    pallas_call x1, Pallas kernels, body(): pl.pallas_call(functools.partial(block_kernel, n_grp, n_dom), out_shape=(...  44.9 us
    pallas_call x1, Pallas kernels, body(): pl.pallas_call(finish_kernel, out_shape=(jax.ShapeDtypeStruct((fine, widt...  2.21 us

profile of v7, /device:TPU:1, one launch (start us, length us, event | category | flops | bytes accessed | tf_op | source)
XLA Modules:
  0.0 47.7 jit_solution(192602127842790156)
XLA Ops:
  0.6 44.9 %block.1 = (f32[2048,128]{1,0:T(8,128)}, f32[768,128]{1,0:T(8,128)}) custom-call(bf16[2048,128]{1,0:T(8,128)(2,1)} %refs_0_.1, bf16[2048,128]{1,0:T(8,128)(2,1)} %refs_1_.1, bf16[128,128]{1,0:T(8,128)(2,1)} %refs_2_.1, bf16[128,128]{1,0:T(8,128)(2,1)} %refs_3_.1, bf16[128,128]{1,0:T(8,128)(2,1)} %refs_4_.1, bf16[128,128]{1,0:T(8,128)(2,1)} %refs_5_.1, ...), custom_call_target="tpu_custom_call" | custom-call | tf_op jit(solution)/shard_map/block/pallas_call | solution.py:560
  45.5 2.2 %finish.1 = (f32[2048,128]{1,0:T(8,128)}, f32[128,128]{1,0:T(8,128)}, f32[128,128]{1,0:T(8,128)}, f32[128,128]{1,0:T(8,128)}, f32[128,128]{1,0:T(8,128)}, /*index=5*/f32[128,128]{1,0:T(8,128)}, f32[128,128]{1,0:T(8,128)}) custom-call(f32[2048,128]{1,0:T(8,128)} %get-tuple-element.9.node_ref, f32[768,128]{1,0:T(8,128)} %get-tuple-element.10.sums_ref), custom_call_target="tpu_custom_call" | custom-call | tf_op jit(solution)/shard_map/finish/pallas_call | solution.py:603
